TPU v7x, 512 devices: a whole 4x4x16 slice. The times are simulated.
512 devices in a mesh: ctx: 128 (over x, z, core), head: 4 (over y).
Axes of the slice: x: 4, y: 4, z: 16, core: 2. Of those that a mesh axis runs over, the one named last changes fastest.
Arguments:
- queries: bfloat16 [16384, 4096], P('ctx', 'head'), may hold values from -6 to 6
- keys: bfloat16 [16384, 4096], P('ctx', 'head'), may hold values from -6 to 6
- values: bfloat16 [16384, 4096], P('ctx', 'head'), may hold values from -60 to 60
- gain: float32 [4096], P('head'), may hold values from 0.1 to 1.9
- cotangent: bfloat16 [16384, 4096], P('ctx', 'head'), may hold values from -6 to 6
Outputs:
- normed: bfloat16 [16384, 4096], P('ctx', 'head')
- grad_queries: bfloat16 [16384, 4096], P('ctx', 'head')
- grad_keys: bfloat16 [16384, 4096], P('ctx', 'head')
- grad_values: bfloat16 [16384, 4096], P('ctx', 'head')
All inputs are finite; a program needn't handle non-finite values.
Results may differ from a plain program's by a relative error of at most 0.0065.
Values may be sent and summed in bfloat16 or wider, within the bound.
No kernel may reach another device: no remote copies, remote signals or barrier semaphores. Data moves between devices by JAX's collectives and lax.ppermute only.
A program may use at most 192 MiB of HBM per device.

v0:
```python
import jax
import jax.numpy as jnp
from jax import lax
from jax.sharding import PartitionSpec as P

HEADS = 32
DH = 128


EPSILON = 1e-06


def entering(part, axis, combine, identity, reverse):
    count = lax.axis_size(axis)
    place = lax.axis_index(axis)
    ahead = count - 1 - place if reverse else place
    gathered = lax.all_gather(part, axis)
    state = jnp.zeros_like(part) + jnp.asarray(identity, part.dtype)

    def one(turn, state):
        source = count - 1 - turn if reverse else turn
        return combine(state, lax.dynamic_index_in_dim(gathered, source, 0, False))

    return lax.fori_loop(0, ahead, one, state)


def add_pair(first, second):
    return first + second


def local(queries, keys, values, gain, cotangent):
    rows_here = queries.shape[0]
    columns = queries.shape[1]
    local_heads = columns // DH
    query_heads = queries.reshape(rows_here, local_heads, DH)
    key_heads = keys.reshape(rows_here, local_heads, DH)
    value_heads = values.reshape(rows_here, local_heads, DH)
    causal = jnp.tril(jnp.ones((rows_here, rows_here), dtype=bool))
    width_all = HEADS * DH
    states = jnp.einsum("tha,thc->hac", key_heads, value_heads, preferred_element_type=jnp.float32)
    before_sum = entering(states, "ctx", add_pair, jnp.zeros_like(states), False)
    before = before_sum.astype(jnp.bfloat16)
    raw = jnp.einsum("tha,sha->hts", query_heads, key_heads, preferred_element_type=jnp.float32)
    scores = jnp.where(causal[None], raw, 0.0).astype(jnp.bfloat16)
    inside = jnp.einsum("hts,shc->thc", scores, value_heads, preferred_element_type=jnp.float32)
    carried = jnp.einsum("tha,hac->thc", query_heads, before, preferred_element_type=jnp.float32)
    attended = (inside + carried).reshape(rows_here, columns)
    squares = lax.psum(jnp.sum(attended * attended, axis=1), "head")
    inverse = lax.rsqrt(squares / width_all + EPSILON)
    normed = (attended * inverse[:, None] * gain).astype(jnp.bfloat16)
    weighted = cotangent.astype(jnp.float32) * gain
    crossed = lax.psum(jnp.sum(weighted * attended, axis=1), "head") / width_all
    grad_attended = (
        inverse[:, None] * weighted - (inverse * inverse * inverse * crossed)[:, None] * attended
    ).astype(jnp.bfloat16)
    grad_heads = grad_attended.reshape(rows_here, local_heads, DH)
    products = jnp.einsum(
        "tha,thc->hac", query_heads, grad_heads, preferred_element_type=jnp.float32
    )
    beyond_sum = entering(products, "ctx", add_pair, jnp.zeros_like(products), True)
    beyond = beyond_sum.astype(jnp.bfloat16)
    raw_grad = jnp.einsum(
        "thc,shc->hts", grad_heads, value_heads, preferred_element_type=jnp.float32
    )
    grad_scores = jnp.where(causal[None], raw_grad, 0.0).astype(jnp.bfloat16)
    grad_q = jnp.einsum("hts,sha->tha", grad_scores, key_heads, preferred_element_type=jnp.float32)
    grad_q = grad_q + jnp.einsum(
        "thc,hac->tha", grad_heads, before, preferred_element_type=jnp.float32
    )
    grad_k = jnp.einsum(
        "hts,tha->sha", grad_scores, query_heads, preferred_element_type=jnp.float32
    )
    grad_k = grad_k + jnp.einsum(
        "shc,hac->sha", value_heads, beyond, preferred_element_type=jnp.float32
    )
    grad_v = jnp.einsum("hts,thc->shc", scores, grad_heads, preferred_element_type=jnp.float32)
    grad_v = grad_v + jnp.einsum(
        "sha,hac->shc", key_heads, beyond, preferred_element_type=jnp.float32
    )
    return (
        normed,
        grad_q.reshape(rows_here, columns).astype(jnp.bfloat16),
        grad_k.reshape(rows_here, columns).astype(jnp.bfloat16),
        grad_v.reshape(rows_here, columns).astype(jnp.bfloat16),
    )


def solution(mesh):
    in_specs = (P("ctx", "head"), P("ctx", "head"), P("ctx", "head"), P("head"), P("ctx", "head"))
    out_specs = (P("ctx", "head"), P("ctx", "head"), P("ctx", "head"), P("ctx", "head"))
    return jax.shard_map(local, mesh=mesh, in_specs=in_specs, out_specs=out_specs, check_vma=False)
```

profile of v0, /device:TPU:1, one launch (start us, length us, event | category | flops | bytes accessed | tf_op | source)
XLA Modules:
  0.0 926.3 jit_solution(4373307273640840020)
XLA Ops:
  9.6 1.3 fusion.3
  11.0 302.7 %all-gather.5.cloned.1.call-done = f32[1024,128,128]{2,1,0:T(8,128)} async-done(((f32[8,128,128]{2,1,0:T(8,128)}), f32[1024,128,128]{2,1,0:T(8,128)}) %all-gather.5.cloned.1.call-update) | async-done | bytes 67108880 | tf_op jit(solution)/shard_map/all_gather | solution.py:17
  313.8 1.2 while.22
  313.8 1.2 bitcast_add_fusion.4
  315.0 1.3 convolution_bitcast_fusion.5
  317.9 8.5 all-reduce
  326.4 1.8 subtract_convert_fusion
  332.3 1.2 convolution_bitcast_fusion
  333.8 432.2 %all-gather.7.cloned.1.call-done = f32[1024,128,128]{2,1,0:T(8,128)} async-done(((f32[8,128,128]{2,1,0:T(8,128)}), f32[1024,128,128]{2,1,0:T(8,128)}) %all-gather.7.cloned.1.call-update) | async-done | bytes 67108880 | tf_op jit(solution)/shard_map/all_gather | solution.py:17
  766.0 150.1 %while.23 = (s32[]{:T(128)}, f32[8,128,128]{2,1,0:T(8,128)S(1)}, s32[]{:T(128)}, f32[128,8,128,128]{3,2,1,0:T(8,128)}, s32[]{:T(128)}, /*index=5*/s32[]{:T(128)}, s32[]{:T(128)}, s32[]{:T(128)}) while((s32[]{:T(128)}, f32[8,128,128]{2,1,0:T(8,128)S(1)}, s32[]{:T(128)}, f32[128,8,128,128]{3,2,1,0:T(8,128)}, s32[]{:T(128)}, ...), condition=%wide.region_7.8_spmd, body=%wide.region_6.7_spmd.sunk | while | flops 131078 | bytes 1573007 | solution.py:24
  770.8 1.2 bitcast_add_fusion.5
  772.0 1.2 bitcast_add_fusion.5
  773.2 1.2 bitcast_add_fusion.5
  774.4 1.2 bitcast_add_fusion.5
  775.6 1.2 bitcast_add_fusion.5
  776.8 1.2 bitcast_add_fusion.5
  778.0 1.2 bitcast_add_fusion.5
  793.4 1.2 bitcast_add_fusion.5
  794.6 1.2 bitcast_add_fusion.5
  795.8 1.2 bitcast_add_fusion.5
  797.0 1.2 bitcast_add_fusion.5
  798.2 1.2 bitcast_add_fusion.5
  799.4 1.2 bitcast_add_fusion.5
  800.6 1.2 bitcast_add_fusion.5
  816.1 1.2 bitcast_add_fusion.5
  817.3 1.2 bitcast_add_fusion.5
  818.5 1.2 bitcast_add_fusion.5
  819.7 1.2 bitcast_add_fusion.5
  820.9 1.2 bitcast_add_fusion.5
  822.0 1.2 bitcast_add_fusion.5
  823.2 1.2 bitcast_add_fusion.5
  838.7 1.2 bitcast_add_fusion.5
  839.9 1.2 bitcast_add_fusion.5
  841.1 1.2 bitcast_add_fusion.5
  842.3 1.2 bitcast_add_fusion.5
  843.5 1.2 bitcast_add_fusion.5
  844.7 1.2 bitcast_add_fusion.5
  845.9 1.2 bitcast_add_fusion.5
  861.4 1.2 bitcast_add_fusion.5
  862.6 1.2 bitcast_add_fusion.5
  863.8 1.2 bitcast_add_fusion.5
  864.9 1.2 bitcast_add_fusion.5
  866.1 1.2 bitcast_add_fusion.5
  867.3 1.2 bitcast_add_fusion.5
  868.5 1.2 bitcast_add_fusion.5
  884.0 1.2 bitcast_add_fusion.5
  885.2 1.2 bitcast_add_fusion.5
  916.5 1.3 fusion.5
  (116 shorter events, 114.5 us)
Async XLA Ops:
  7.2 1.3 copy-start
  7.2 306.5 %all-gather.5.cloned.1.call-start = ((), (), s32[]{:S(2)}) async-start(), calls=%async_computation | async-start | bytes 67633152 | tf_op jit(solution)/shard_map/all_gather | solution.py:17
  9.6 756.4 %all-gather.7.cloned.1.call-start = ((), (), s32[]{:S(2)}) async-start(), calls=%async_computation.1 | async-start | bytes 67633152 | tf_op jit(solution)/shard_map/all_gather | solution.py:17
Sparse Core Ops, SparseCore 0:
  11.2 302.5 all-gather.4
  330.7 435.2 all-gather.6
where the time goes:
time: 933 us; the launch traced here: 926 us
  waiting for transfers between devices  735 us (79%)
  other arithmetic  151 us (16%)
  between operations  14.2 us (2%)
    all_gather x2, waiting for transfers between devices, entering(): gathered = lax.all_gather(part, axis)  735 us
    add x127, other arithmetic, add_pair(): return first + second  148 us
  transfers between devices with their start and end apart: 2, of which 2 were waited for; matrix products, arithmetic and copies ran while one was open for 0% of the time, Pallas kernels for 0%

commit v1 on v0

v1 whole, which is shorter than its diff:
```python
import jax
import jax.numpy as jnp
from jax import lax
from jax.experimental import pallas as pl
from jax.experimental.pallas import tpu as pltpu
from jax.sharding import Mesh, PartitionSpec as P

HEADS = 32
DH = 128
ROWS = 128
LOCAL = 8
HALF = LOCAL // 2
WIDTH = LOCAL * DH
WIDTH_ALL = HEADS * DH
EPSILON = 1e-06
X, Z, CORES, GROUPS = 4, 16, 2, 4
CHIPS = X * Z
PIECE = HALF * DH // CHIPS
F32 = jnp.float32
BF16 = jnp.bfloat16

VMEM = pl.BlockSpec(memory_space=pltpu.VMEM)
SMEM = pl.BlockSpec(memory_space=pltpu.SMEM)


def dot(a, b, ca, cb):
    return lax.dot_general(a, b, (((ca,), (cb,)), ((), ())), preferred_element_type=F32)


def head(ref, h):
    return ref[:, h * DH : (h + 1) * DH]


def causal():
    t = lax.broadcasted_iota(jnp.int32, (ROWS, ROWS), 0)
    s = lax.broadcasted_iota(jnp.int32, (ROWS, ROWS), 1)
    return s <= t


def call(kernel, shapes, flops, moved, specs):
    return pl.pallas_call(
        kernel,
        out_shape=[jax.ShapeDtypeStruct(s, d) for s, d in shapes],
        in_specs=specs,
        out_specs=[VMEM] * len(shapes),
        compiler_params=pltpu.CompilerParams(vmem_limit_bytes=32 * 1024 * 1024),
        cost_estimate=pl.CostEstimate(flops=flops, bytes_accessed=moved, transcendentals=0),
    )


MATMUL = LOCAL * 2 * DH * DH * DH
BLOCK = ROWS * WIDTH * 2


def states_kernel(k_ref, v_ref, s_ref, sent_ref):
    for h in range(LOCAL):
        state = dot(head(k_ref, h), head(v_ref, h), 0, 0)
        s_ref[h] = state
        sent_ref[h] = state.astype(BF16)


def pair_kernel(core_ref, own_ref, pair_ref, out_ref):
    other = 1 - core_ref[0]
    half = core_ref[0] * HALF
    for h in range(HALF):
        out_ref[h * DH : (h + 1) * DH, :] = (own_ref[half + h] + pair_ref[other, half + h].astype(F32)).astype(BF16)


def prefix_kernel(in_ref, out_ref):
    total = jnp.zeros((PIECE, DH), F32)
    for i in range(CHIPS // 2):
        two = in_ref[i * 2 * PIECE : (i + 1) * 2 * PIECE, :].astype(F32)
        middle = total + two[:PIECE]
        out_ref[i * 2 * PIECE : (i + 1) * 2 * PIECE, :] = jnp.concatenate([total, middle], axis=0).astype(BF16)
        total = middle + two[PIECE:]


def suffix_kernel(in_ref, out_ref):
    total = jnp.zeros((PIECE, DH), F32)
    for i in reversed(range(CHIPS // 2)):
        two = in_ref[i * 2 * PIECE : (i + 1) * 2 * PIECE, :].astype(F32)
        middle = total + two[PIECE:]
        out_ref[i * 2 * PIECE : (i + 1) * 2 * PIECE, :] = jnp.concatenate([middle, total], axis=0).astype(BF16)
        total = middle + two[:PIECE]


def inside_kernel(q_ref, k_ref, v_ref, scores_ref, inside_ref):
    mask = causal()
    for h in range(LOCAL):
        raw = dot(head(q_ref, h), head(k_ref, h), 1, 1)
        scores = jnp.where(mask, raw, 0.0).astype(BF16)
        scores_ref[h] = scores
        inside_ref[:, h * DH : (h + 1) * DH] = dot(scores, head(v_ref, h), 1, 0)


def attended_kernel(core_ref, q_ref, inside_ref, chips_ref, pair_ref, c_ref, gain_ref, att_ref, before_ref, sums_ref):
    second = core_ref[0] == 1
    squares = jnp.zeros((ROWS, DH), F32)
    crossed = jnp.zeros((ROWS, DH), F32)
    for h in range(LOCAL):
        other = jnp.where(second, pair_ref[0, h].astype(F32), 0.0)
        before = (chips_ref[h * DH : (h + 1) * DH, :].astype(F32) + other).astype(BF16)
        before_ref[h] = before
        att = head(inside_ref, h) + dot(head(q_ref, h), before, 1, 0)
        att_ref[:, h * DH : (h + 1) * DH] = att
        weighted = head(c_ref, h).astype(F32) * gain_ref[:, h * DH : (h + 1) * DH]
        squares = squares + att * att
        crossed = crossed + weighted * att
    row0 = jnp.sum(squares.T, axis=0, keepdims=True)
    row1 = jnp.sum(crossed.T, axis=0, keepdims=True)
    block = jnp.concatenate([row0, row1, jnp.zeros((6, ROWS), F32)], axis=0)
    for i in range(GROUPS):
        sums_ref[i * 8 : (i + 1) * 8, :] = block


def grad_kernel(sums_ref, att_ref, q_ref, c_ref, gain_ref, normed_ref, g_ref, products_ref, sent_ref):
    sums = sums_ref[0:8, :]
    for i in range(1, GROUPS):
        sums = sums + sums_ref[i * 8 : (i + 1) * 8, :]
    inverse_row = lax.rsqrt(sums[0:1] / WIDTH_ALL + EPSILON)
    cubed_row = inverse_row * inverse_row * inverse_row * (sums[1:2] / WIDTH_ALL)
    inverse = jnp.broadcast_to(inverse_row, (ROWS, ROWS)).T
    cubed = jnp.broadcast_to(cubed_row, (ROWS, ROWS)).T
    for h in range(LOCAL):
        at = slice(h * DH, (h + 1) * DH)
        att = att_ref[:, at]
        gain = gain_ref[:, at]
        normed_ref[:, at] = (att * inverse * gain).astype(BF16)
        weighted = c_ref[:, at].astype(F32) * gain
        g = (inverse * weighted - cubed * att).astype(BF16)
        g_ref[:, at] = g
        product = dot(q_ref[:, at], g, 0, 0)
        products_ref[h] = product
        sent_ref[h] = product.astype(BF16)


def local_grads_kernel(q_ref, k_ref, v_ref, g_ref, scores_ref, before_ref, gq_ref, gk_ref, gv_ref):
    mask = causal()
    for h in range(LOCAL):
        at = slice(h * DH, (h + 1) * DH)
        g = g_ref[:, at]
        raw = dot(g, v_ref[:, at], 1, 1)
        grad_scores = jnp.where(mask, raw, 0.0).astype(BF16)
        gq = dot(grad_scores, k_ref[:, at], 1, 0) + dot(g, before_ref[h], 1, 1)
        gq_ref[:, at] = gq.astype(BF16)
        gk_ref[:, at] = dot(grad_scores, q_ref[:, at], 0, 0)
        gv_ref[:, at] = dot(scores_ref[h], g, 0, 0)


def final_kernel(core_ref, k_ref, v_ref, gk_part_ref, gv_part_ref, chips_ref, pair_ref, gk_ref, gv_ref):
    first = core_ref[0] == 0
    for h in range(LOCAL):
        at = slice(h * DH, (h + 1) * DH)
        other = jnp.where(first, pair_ref[1, h].astype(F32), 0.0)
        beyond = (chips_ref[at, :].astype(F32) + other).astype(BF16)
        gk_ref[:, at] = (gk_part_ref[:, at] + dot(v_ref[:, at], beyond, 1, 1)).astype(BF16)
        gv_ref[:, at] = (gv_part_ref[:, at] + dot(k_ref[:, at], beyond, 1, 0)).astype(BF16)


STATE = (LOCAL, DH, DH)
FLAT = (HALF * DH, DH)


def chips_scan(core, own, pair, kernel):
    (mine,) = call(pair_kernel, [(FLAT, BF16)], 0, 4 * BLOCK, [SMEM, VMEM, VMEM])(core, own, pair)
    turned = lax.all_to_all(mine, ("x", "z"), 0, 0, tiled=True)
    (summed,) = call(kernel, [(FLAT, BF16)], 0, BLOCK, [VMEM])(turned)
    back = lax.all_to_all(summed, ("x", "z"), 0, 0, tiled=True)
    return lax.all_gather(back, "core", axis=0, tiled=True)


def local(q, k, v, gain, c):
    core = lax.axis_index("core").reshape(1).astype(jnp.int32)
    gain = gain.reshape(1, WIDTH)
    states, sent = call(states_kernel, [(STATE, F32), (STATE, BF16)], MATMUL, 5 * BLOCK, [VMEM] * 2)(k, v)
    pair = lax.all_gather(sent, "core")
    scores, inside = call(
        inside_kernel, [(STATE, BF16), ((ROWS, WIDTH), F32)], 2 * MATMUL, 6 * BLOCK, [VMEM] * 3
    )(q, k, v)
    chips = chips_scan(core, states, pair, prefix_kernel)
    att, before, sums = call(
        attended_kernel,
        [((ROWS, WIDTH), F32), (STATE, BF16), ((GROUPS * 8, ROWS), F32)],
        MATMUL, 10 * BLOCK, [SMEM] + [VMEM] * 6,
    )(core, q, inside, chips, pair, c, gain)
    sums = lax.all_to_all(sums, "head", 0, 0, tiled=True)
    normed, g, products, sent2 = call(
        grad_kernel,
        [((ROWS, WIDTH), BF16), ((ROWS, WIDTH), BF16), (STATE, F32), (STATE, BF16)],
        MATMUL, 10 * BLOCK, [VMEM] * 5,
    )(sums, att, q, c, gain)
    pair2 = lax.all_gather(sent2, "core")
    gq, gk_part, gv_part = call(
        local_grads_kernel,
        [((ROWS, WIDTH), BF16), ((ROWS, WIDTH), F32), ((ROWS, WIDTH), F32)],
        5 * MATMUL, 11 * BLOCK, [VMEM] * 6,
    )(q, k, v, g, scores, before)
    chips2 = chips_scan(core, products, pair2, suffix_kernel)
    gk, gv = call(
        final_kernel, [((ROWS, WIDTH), BF16), ((ROWS, WIDTH), BF16)], 2 * MATMUL, 12 * BLOCK, [SMEM] + [VMEM] * 6
    )(core, k, v, gk_part, gv_part, chips2, pair2)
    return normed, gq, gk, gv


def solution(mesh):
    fine = Mesh(mesh.devices.reshape(X, Z, CORES, GROUPS), ("x", "z", "core", "head"))
    block = P(("x", "z", "core"), "head")
    return jax.shard_map(
        local, mesh=fine, in_specs=(block, block, block, P("head"), block), out_specs=(block,) * 4, check_vma=False
    )
```

time: 933 us -> 127 us (0.14)
  waiting for transfers between devices: 735 us -> 24.7 us
  other arithmetic: 151 us -> 0 us
  blocking collectives: 8.46 us -> 77.2 us
  starting transfers between devices: 0.08 us -> 14.5 us
  between operations: 14.2 us -> 0.73 us
    all_gather x2 -> x0, waiting for transfers between devices: 735 us -> none  [entering(): gathered = lax.all_gather(part, axis)]
    add x127 -> x0, other arithmetic: 148 us -> none  [add_pair(): return first + second]
    all_to_all x0 -> x3, blocking collectives: none -> 55 us  [the longest x2 46.8 us: chips_scan(): turned = lax.all_to_all(mine, ('x', 'z'), 0, 0, tiled=True)]
    all_to_all x0 -> x2, waiting for transfers between devices: none -> 24.7 us  [chips_scan(): back = lax.all_to_all(summed, ('x', 'z'), 0, 0, tiled=True)]
    all_gather x0 -> x4, blocking collectives: none -> 22.2 us  [the longest x2 9.95 us: chips_scan(): return lax.all_gather(back, 'core', axis=0, tiled=True)]
    all_to_all x0 -> x2, starting transfers between devices: none -> 14.5 us  [chips_scan(): back = lax.all_to_all(summed, ('x', 'z'), 0, 0, tiled=True)]
  transfers between devices with their start and end apart: 2 -> 2, of which waited for: 2 -> 2; matrix products, arithmetic and copies ran while one was open for 0% -> 0% of each run, Pallas kernels for 0% -> 3%
where the time goes in v1:
time: 127 us
  blocking collectives  77.2 us (61%)
  waiting for transfers between devices  24.7 us (19%)
  starting transfers between devices  14.5 us (11%)
  Pallas kernels  7.66 us (6%)
  local copies, waits for them, and re-layouts  1.92 us (2%)
    all_to_all x2, blocking collectives, chips_scan(): turned = lax.all_to_all(mine, ('x', 'z'), 0, 0, tiled=True)  46.8 us
    all_to_all x2, waiting for transfers between devices, chips_scan(): back = lax.all_to_all(summed, ('x', 'z'), 0, 0, tiled=True)  24.7 us
    all_to_all x2, starting transfers between devices, chips_scan(): back = lax.all_to_all(summed, ('x', 'z'), 0, 0, tiled=True)  14.5 us
    all_gather x2, blocking collectives, chips_scan(): return lax.all_gather(back, 'core', axis=0, tiled=True)  9.95 us
    all_gather x1, blocking collectives, local(): pair = lax.all_gather(sent, 'core')  8.68 us
    all_to_all x1, blocking collectives, local(): sums = lax.all_to_all(sums, 'head', 0, 0, tiled=True)  8.2 us
    all_gather x1, blocking collectives, local(): pair2 = lax.all_gather(sent2, 'core')  3.59 us
  transfers between devices with their start and end apart: 2, of which 2 were waited for; matrix products, arithmetic and copies ran while one was open for 0% of the time, Pallas kernels for 3%

profile of v1, /device:TPU:1, one launch (start us, length us, event | category | flops | bytes accessed | tf_op | source)
XLA Modules:
  0.0 126.7 jit_solution(1253367865553999818)
XLA Ops:
  0.6 0.0 copy-start
  0.6 0.9 copy-done
  1.6 0.0 copy-start.2
  1.6 0.9 copy-done.2
  2.5 0.3 shard_map.85
  2.8 8.7 %all-gather = bf16[16,128,128]{2,1,0:T(8,128)(2,1)S(1)} all-gather(bf16[8,128,128]{2,1,0:T(8,128)(2,1)S(1)} %get-tuple-element.22), channel_id=2, replica_groups=mesh['x'=4,'z'=16,'core'=2,'head'=4] {'core'}, dimensions={0}, use_global_device_ids=true | all-gather | bytes 786432 | tf_op jit(solution)/shard_map/all_gather | solution.py:176
  11.5 0.0 copy-start.4
  11.5 27.3 %all_to_all.57 = bf16[64,8,128]{2,1,0:T(8,128)(2,1)S(1)} all-to-all(bf16[64,8,128]{2,1,0:T(8,128)(2,1)S(1)} %bitcast.18), channel_id=1, replica_groups=mesh['x'=4,'z'=16,'core'=2,'head'=4] {'x','z'}, dimensions={0} | all-to-all | bytes 262144 | tf_op jit(solution)/shard_map/all_to_all | solution.py:166
  38.8 0.0 copy-start.1
  38.8 0.0 copy-start.3
  38.8 0.7 shard_map.87
  39.5 7.3 %all-to-all-start.1 = ((bf16[64,8,128]{2,1,0:T(8,128)(2,1)}), bf16[64,8,128]{2,1,0:T(8,128)(2,1)S(1)}, u32[]{:S(2)}, u32[]{:S(2)}) async-start(bf16[64,8,128]{2,1,0:T(8,128)(2,1)} %bitcast.4), calls=%async_computation.1 | async-start | bytes 262144 | tf_op jit(solution)/shard_map/all_to_all | solution.py:168
  46.8 0.0 copy-done.4
  46.8 0.0 copy-done.1
  46.8 0.0 copy-done.3
  46.8 1.3 %shard_map.84 = (bf16[8,128,128]{2,1,0:T(8,128)(2,1)S(1)}, f32[128,1024]{1,0:T(8,128)S(1)}) custom-call(bf16[128,1024]{1,0:T(8,128)(2,1)S(1)} %copy-done.4, bf16[128,1024]{1,0:T(8,128)(2,1)S(1)} %copy-done.1, bf16[128,1024]{1,0:T(8,128)(2,1)S(1)} %copy-done.3), custom_call_target="tpu_custom_call" | custom-call | flops 67108864 | bytes 1572864 | tf_op jit(solution)/shard_map/pallas_call | solution.py:177
  48.2 0.0 copy-start.5
  48.2 12.7 %all-to-all-done.1 = bf16[64,8,128]{2,1,0:T(8,128)(2,1)S(1)} async-done(((bf16[64,8,128]{2,1,0:T(8,128)(2,1)}), bf16[64,8,128]{2,1,0:T(8,128)(2,1)S(1)}, u32[]{:S(2)}, u32[]{:S(2)}) %all-to-all-start.1) | async-done | bytes 131104 | tf_op jit(solution)/shard_map/all_to_all | solution.py:168
  60.9 0.0 copy-start.6
  60.9 5.0 %all_gather.20.chips_ref = bf16[1024,128]{1,0:T(8,128)(2,1)S(1)} all-gather(bf16[512,128]{1,0:T(8,128)(2,1)S(1)} %bitcast.27), channel_id=1, replica_groups=mesh['x'=4,'z'=16,'core'=2,'head'=4] {'core'}, dimensions={0}, use_global_device_ids=true | all-gather | bytes 393216 | tf_op jit(solution)/shard_map/all_gather | solution.py:169
  65.9 0.0 copy-done.5
  65.9 0.0 copy-done.6
  65.9 0.3 shard_map.88
  66.3 8.2 %all_to_all.58 = f32[4,8,128]{2,1,0:T(8,128)S(1)} all-to-all(f32[4,8,128]{2,1,0:T(8,128)S(1)} %bitcast.25), channel_id=1, replica_groups=mesh['x'=4,'z'=16,'core'=2,'head'=4] {'head'}, dimensions={0} | all-to-all | bytes 32768 | tf_op jit(solution)/shard_map/all_to_all | solution.py:186
  74.5 1.0 shard_map.89
  75.5 3.6 %all-gather.1 = bf16[16,128,128]{2,1,0:T(8,128)(2,1)S(1)} all-gather(bf16[8,128,128]{2,1,0:T(8,128)(2,1)S(1)} %get-tuple-element.33), channel_id=3, replica_groups=mesh['x'=4,'z'=16,'core'=2,'head'=4] {'core'}, dimensions={0}, use_global_device_ids=true | all-gather | bytes 786432 | tf_op jit(solution)/shard_map/all_gather | solution.py:192
  79.1 19.5 %all_to_all.59 = bf16[64,8,128]{2,1,0:T(8,128)(2,1)S(1)} all-to-all(bf16[64,8,128]{2,1,0:T(8,128)(2,1)S(1)} %bitcast.19), channel_id=1, replica_groups=mesh['x'=4,'z'=16,'core'=2,'head'=4] {'x','z'}, dimensions={0} | all-to-all | bytes 262144 | tf_op jit(solution)/shard_map/all_to_all | solution.py:166
  98.6 0.7 shard_map.92
  99.3 7.3 %all-to-all-start.4 = ((bf16[64,8,128]{2,1,0:T(8,128)(2,1)}), bf16[64,8,128]{2,1,0:T(8,128)(2,1)S(1)}, u32[]{:S(2)}, u32[]{:S(2)}) async-start(bf16[64,8,128]{2,1,0:T(8,128)(2,1)} %bitcast.12), calls=%async_computation.4 | async-start | bytes 262144 | tf_op jit(solution)/shard_map/all_to_all | solution.py:168
  106.6 2.1 %shard_map.90 = (bf16[128,1024]{1,0:T(8,128)(2,1)}, f32[128,1024]{1,0:T(8,128)S(1)}, f32[128,1024]{1,0:T(8,128)S(1)}) custom-call(bf16[128,1024]{1,0:T(8,128)(2,1)S(1)} %copy-done.4, bf16[128,1024]{1,0:T(8,128)(2,1)S(1)} %copy-done.1, bf16[128,1024]{1,0:T(8,128)(2,1)S(1)} %copy-done.3, bf16[128,1024]{1,0:T(8,128)(2,1)S(1)} %get-tuple-element.26.g_ref, ...), custom_call_target="tpu_custom_call" | custom-call | flops 167772160 | bytes 2883584 | tf_op jit(solution)/shard_map/pallas_call | solution.py:193
  108.6 12.0 %all-to-all-done.4 = bf16[64,8,128]{2,1,0:T(8,128)(2,1)S(1)} async-done(((bf16[64,8,128]{2,1,0:T(8,128)(2,1)}), bf16[64,8,128]{2,1,0:T(8,128)(2,1)S(1)}, u32[]{:S(2)}, u32[]{:S(2)}) %all-to-all-start.4) | async-done | bytes 131104 | tf_op jit(solution)/shard_map/all_to_all | solution.py:168
  120.6 4.9 %all_gather.23.chips_ref = bf16[1024,128]{1,0:T(8,128)(2,1)S(1)} all-gather(bf16[512,128]{1,0:T(8,128)(2,1)S(1)} %bitcast.26), channel_id=1, replica_groups=mesh['x'=4,'z'=16,'core'=2,'head'=4] {'core'}, dimensions={0}, use_global_device_ids=true | all-gather | bytes 393216 | tf_op jit(solution)/shard_map/all_gather | solution.py:169
  125.5 1.2 shard_map.93
  (2 shorter events, 0.1 us)
Async XLA Ops:
  0.6 1.0 copy-start
  1.6 0.9 copy-start.2
  11.5 35.3 %copy-start.4 = (bf16[128,1024]{1,0:T(8,128)(2,1)S(1)}, bf16[128,1024]{1,0:T(8,128)(2,1)}, u32[]{:S(2)}) copy-start(bf16[128,1024]{1,0:T(8,128)(2,1)} %q_ref.7) | copy-start | bytes 786436
  38.8 8.0 %copy-start.1 = (bf16[128,1024]{1,0:T(8,128)(2,1)S(1)}, bf16[128,1024]{1,0:T(8,128)(2,1)}, u32[]{:S(2)}) copy-start(bf16[128,1024]{1,0:T(8,128)(2,1)} %k_ref.7) | copy-start | bytes 786436
  38.8 8.0 %copy-start.3 = (bf16[128,1024]{1,0:T(8,128)(2,1)S(1)}, bf16[128,1024]{1,0:T(8,128)(2,1)}, u32[]{:S(2)}) copy-start(bf16[128,1024]{1,0:T(8,128)(2,1)} %v_ref.7) | copy-start | bytes 786436
  39.5 21.3 %all-to-all-start.1 = ((bf16[64,8,128]{2,1,0:T(8,128)(2,1)}), bf16[64,8,128]{2,1,0:T(8,128)(2,1)S(1)}, u32[]{:S(2)}, u32[]{:S(2)}) async-start(bf16[64,8,128]{2,1,0:T(8,128)(2,1)} %bitcast.4), calls=%async_computation.1 | async-start | bytes 262144 | tf_op jit(solution)/shard_map/all_to_all | solution.py:168
  48.2 17.7 %copy-start.5 = (bf16[128,1024]{1,0:T(8,128)(2,1)S(1)}, bf16[128,1024]{1,0:T(8,128)(2,1)}, u32[]{:S(2)}) copy-start(bf16[128,1024]{1,0:T(8,128)(2,1)} %c_ref.3) | copy-start | bytes 786436
  60.9 5.0 %copy-start.6 = (f32[1024]{0:T(1024)S(1)}, f32[1024]{0:T(1024)}, u32[]{:S(2)}) copy-start(f32[1024]{0:T(1024)} %param.8) | copy-start | bytes 12292
  99.3 21.3 %all-to-all-start.4 = ((bf16[64,8,128]{2,1,0:T(8,128)(2,1)}), bf16[64,8,128]{2,1,0:T(8,128)(2,1)S(1)}, u32[]{:S(2)}, u32[]{:S(2)}) async-start(bf16[64,8,128]{2,1,0:T(8,128)(2,1)} %bitcast.12), calls=%async_computation.4 | async-start | bytes 262144 | tf_op jit(solution)/shard_map/all_to_all | solution.py:168

commit v2 on v1

--- a/solution.py
+++ b/solution.py
@@ -1,3 +1,5 @@
+import functools
+
 import jax
 import jax.numpy as jnp
 from jax import lax
@@ -13,9 +15,8 @@
 WIDTH = LOCAL * DH
 WIDTH_ALL = HEADS * DH
 EPSILON = 1e-06
-X, Z, CORES, GROUPS = 4, 16, 2, 4
-CHIPS = X * Z
-PIECE = HALF * DH // CHIPS
+X, ZH, ZL, CORES, GROUPS = 4, 4, 4, 2, 4
+PIECE = HALF * DH // (X * ZL)
 F32 = jnp.float32
 BF16 = jnp.bfloat16
 
@@ -66,22 +67,36 @@
         out_ref[h * DH : (h + 1) * DH, :] = (own_ref[half + h] + pair_ref[other, half + h].astype(F32)).astype(BF16)
 
 
-def prefix_kernel(in_ref, out_ref):
-    total = jnp.zeros((PIECE, DH), F32)
-    for i in range(CHIPS // 2):
-        two = in_ref[i * 2 * PIECE : (i + 1) * 2 * PIECE, :].astype(F32)
-        middle = total + two[:PIECE]
-        out_ref[i * 2 * PIECE : (i + 1) * 2 * PIECE, :] = jnp.concatenate([total, middle], axis=0).astype(BF16)
-        total = middle + two[PIECE:]
-
-
-def suffix_kernel(in_ref, out_ref):
-    total = jnp.zeros((PIECE, DH), F32)
-    for i in reversed(range(CHIPS // 2)):
-        two = in_ref[i * 2 * PIECE : (i + 1) * 2 * PIECE, :].astype(F32)
-        middle = total + two[PIECE:]
-        out_ref[i * 2 * PIECE : (i + 1) * 2 * PIECE, :] = jnp.concatenate([middle, total], axis=0).astype(BF16)
-        total = middle + two[:PIECE]
+def piece(ref, i):
+    return ref[i * PIECE : (i + 1) * PIECE, :].astype(F32)
+
+
+def cube_kernel(in_ref, out_ref):
+    for x in range(X):
+        total = piece(in_ref, x * ZL)
+        for z in range(1, ZL):
+            total = total + piece(in_ref, x * ZL + z)
+        total = total.astype(BF16)
+        for copy in range(ZH):
+            at = (copy * X + x) * PIECE
+            out_ref[at : at + PIECE, :] = total
+
+
+def scan_kernel(reverse, place_ref, in_ref, cubes_ref, out_ref):
+    here = place_ref[0]
+    order = (lambda n: reversed(range(n))) if reverse else range
+    column = jnp.zeros((PIECE, DH), F32)
+    for x in order(X):
+        total = column
+        for z in range(ZH):
+            cube = piece(cubes_ref, z * X + x)
+            column = column + cube
+            ahead = here < z if reverse else here > z
+            total = total + jnp.where(ahead, cube, 0.0)
+        for z in order(ZL):
+            at = (x * ZL + z) * PIECE
+            out_ref[at : at + PIECE, :] = total.astype(BF16)
+            total = total + piece(in_ref, x * ZL + z)
 
 
 def inside_kernel(q_ref, k_ref, v_ref, scores_ref, inside_ref):
@@ -161,11 +176,15 @@
 FLAT = (HALF * DH, DH)
 
 
-def chips_scan(core, own, pair, kernel):
+def chips_scan(core, own, pair, reverse):
     (mine,) = call(pair_kernel, [(FLAT, BF16)], 0, 4 * BLOCK, [SMEM, VMEM, VMEM])(core, own, pair)
-    turned = lax.all_to_all(mine, ("x", "z"), 0, 0, tiled=True)
-    (summed,) = call(kernel, [(FLAT, BF16)], 0, BLOCK, [VMEM])(turned)
-    back = lax.all_to_all(summed, ("x", "z"), 0, 0, tiled=True)
+    place = lax.axis_index("zh").reshape(1).astype(jnp.int32)
+    turned = lax.all_to_all(mine, ("x", "zl"), 0, 0, tiled=True)
+    (cube,) = call(cube_kernel, [(FLAT, BF16)], 0, BLOCK, [VMEM])(turned)
+    cubes = lax.all_to_all(cube, "zh", 0, 0, tiled=True)
+    scan = functools.partial(scan_kernel, reverse)
+    (summed,) = call(scan, [(FLAT, BF16)], 0, 2 * BLOCK, [SMEM, VMEM, VMEM])(place, turned, cubes)
+    back = lax.all_to_all(summed, ("x", "zl"), 0, 0, tiled=True)
     return lax.all_gather(back, "core", axis=0, tiled=True)
 
 
@@ -177,7 +196,7 @@
     scores, inside = call(
         inside_kernel, [(STATE, BF16), ((ROWS, WIDTH), F32)], 2 * MATMUL, 6 * BLOCK, [VMEM] * 3
     )(q, k, v)
-    chips = chips_scan(core, states, pair, prefix_kernel)
+    chips = chips_scan(core, states, pair, False)
     att, before, sums = call(
         attended_kernel,
         [((ROWS, WIDTH), F32), (STATE, BF16), ((GROUPS * 8, ROWS), F32)],
@@ -195,7 +214,7 @@
         [((ROWS, WIDTH), BF16), ((ROWS, WIDTH), F32), ((ROWS, WIDTH), F32)],
         5 * MATMUL, 11 * BLOCK, [VMEM] * 6,
     )(q, k, v, g, scores, before)
-    chips2 = chips_scan(core, products, pair2, suffix_kernel)
+    chips2 = chips_scan(core, products, pair2, True)
     gk, gv = call(
         final_kernel, [((ROWS, WIDTH), BF16), ((ROWS, WIDTH), BF16)], 2 * MATMUL, 12 * BLOCK, [SMEM] + [VMEM] * 6
     )(core, k, v, gk_part, gv_part, chips2, pair2)
@@ -203,8 +222,8 @@
 
 
 def solution(mesh):
-    fine = Mesh(mesh.devices.reshape(X, Z, CORES, GROUPS), ("x", "z", "core", "head"))
-    block = P(("x", "z", "core"), "head")
+    fine = Mesh(mesh.devices.reshape(X, ZH, ZL, CORES, GROUPS), ("x", "zh", "zl", "core", "head"))
+    block = P(("x", "zh", "zl", "core"), "head")
     return jax.shard_map(
         local, mesh=fine, in_specs=(block, block, block, P("head"), block), out_specs=(block,) * 4, check_vma=False
     )

time: 127 us -> 125 us (0.984)
  blocking collectives: 77.2 us -> 69.6 us
  starting transfers between devices: 14.5 us -> 19.3 us
    all_to_all x2 -> x3, blocking collectives: 46.8 us -> 35.6 us  [the longest x2 19.7 us: chips_scan(): turned = lax.all_to_all(mine, ('x', 'zl'), 0, 0, tiled=True)]
    all_to_all x2 -> x3, starting transfers between devices: 14.5 us -> 19.3 us  [the longest x1 12.2 us: chips_scan(): cubes = lax.all_to_all(cube, 'zh', 0, 0, tiled=True)]
    all_gather x2, blocking collectives: 9.95 us -> 13.5 us  [chips_scan(): return lax.all_gather(back, 'core', axis=0, tiled=True)]
    all_to_all x2 -> x3, waiting for transfers between devices: 24.7 us -> 24.1 us  [the longest x1 13.1 us: chips_scan(): cubes = lax.all_to_all(cube, 'zh', 0, 0, tiled=True)]
  transfers between devices with their start and end apart: 2 -> 3, of which waited for: 2 -> 3; matrix products, arithmetic and copies ran while one was open for 0% -> 0% of each run, Pallas kernels for 3% -> 3%
where the time goes in v2:
time: 125 us; the launch traced here: 124 us
  blocking collectives  69.6 us (56%)
  waiting for transfers between devices  24.1 us (19%)
  starting transfers between devices  19.3 us (15%)
  Pallas kernels  8.32 us (7%)
  local copies, waits for them, and re-layouts  1.92 us (2%)
    all_to_all x2, blocking collectives, chips_scan(): turned = lax.all_to_all(mine, ('x', 'zl'), 0, 0, tiled=True)  19.7 us
    all_to_all x1, blocking collectives, chips_scan(): cubes = lax.all_to_all(cube, 'zh', 0, 0, tiled=True)  15.9 us
    all_gather x2, blocking collectives, chips_scan(): return lax.all_gather(back, 'core', axis=0, tiled=True)  13.5 us
    all_to_all x1, waiting for transfers between devices, chips_scan(): cubes = lax.all_to_all(cube, 'zh', 0, 0, tiled=True)  13.1 us
    all_to_all x1, starting transfers between devices, chips_scan(): cubes = lax.all_to_all(cube, 'zh', 0, 0, tiled=True)  12.2 us
    all_to_all x2, waiting for transfers between devices, chips_scan(): back = lax.all_to_all(summed, ('x', 'zl'), 0, 0, tiled=True)  10.9 us
    all_gather x1, blocking collectives, local(): pair = lax.all_gather(sent, 'core')  8.68 us
    all_to_all x1, blocking collectives, local(): sums = lax.all_to_all(sums, 'head', 0, 0, tiled=True)  8.2 us
  transfers between devices with their start and end apart: 3, of which 3 were waited for; matrix products, arithmetic and copies ran while one was open for 0% of the time, Pallas kernels for 3%

profile of v2, /device:TPU:1, one launch (start us, length us, event | category | flops | bytes accessed | tf_op | source)
XLA Modules:
  0.0 123.9 jit_solution(12951923385143228469)
XLA Ops:
  0.6 0.0 copy-start
  0.6 0.9 copy-done
  1.6 0.0 copy-start.2
  1.6 0.9 copy-done.2
  2.5 0.3 shard_map.85
  2.8 8.7 %all-gather = bf16[16,128,128]{2,1,0:T(8,128)(2,1)S(1)} all-gather(bf16[8,128,128]{2,1,0:T(8,128)(2,1)S(1)} %get-tuple-element.22), channel_id=2, replica_groups=mesh['x'=4,'zh'=4,'zl'=4,'core'=2,'head'=4] {'core'}, dimensions={0}, use_global_device_ids=true | all-gather | bytes 786432 | tf_op jit(solution)/shard_map/all_gather | solution.py:195
  11.5 9.9 %all_to_all.79 = bf16[16,32,128]{2,1,0:T(8,128)(2,1)S(1)} all-to-all(bf16[16,32,128]{2,1,0:T(8,128)(2,1)S(1)} %bitcast.27), channel_id=1, replica_groups=mesh['x'=4,'zh'=4,'zl'=4,'core'=2,'head'=4] {'x','zl'}, dimensions={0} | all-to-all | bytes 262144 | tf_op jit(solution)/shard_map/all_to_all | solution.py:182
  21.4 0.7 shard_map.87
  22.1 0.0 copy-start.4
  22.1 12.2 %all-to-all-start.1 = ((bf16[4,128,128]{2,1,0:T(8,128)(2,1)}), bf16[4,128,128]{2,1,0:T(8,128)(2,1)S(1)}, u32[]{:S(2)}, u32[]{:S(2)}) async-start(bf16[4,128,128]{2,1,0:T(8,128)(2,1)} %bitcast.5), calls=%async_computation.1 | async-start | bytes 262144 | tf_op jit(solution)/shard_map/all_to_all | solution.py:184
  34.3 13.1 %all-to-all-done.1 = bf16[4,128,128]{2,1,0:T(8,128)(2,1)S(1)} async-done(((bf16[4,128,128]{2,1,0:T(8,128)(2,1)}), bf16[4,128,128]{2,1,0:T(8,128)(2,1)S(1)}, u32[]{:S(2)}, u32[]{:S(2)}) %all-to-all-start.1) | async-done | bytes 131104 | tf_op jit(solution)/shard_map/all_to_all | solution.py:184
  47.4 0.0 copy-start.1
  47.5 0.0 copy-start.3
  47.5 0.7 shard_map.88
  48.2 3.5 %all-to-all-start.2 = ((bf16[16,32,128]{2,1,0:T(8,128)(2,1)}), bf16[16,32,128]{2,1,0:T(8,128)(2,1)S(1)}, u32[]{:S(2)}, u32[]{:S(2)}) async-start(bf16[16,32,128]{2,1,0:T(8,128)(2,1)} %bitcast.7), calls=%async_computation.2 | async-start | bytes 262144 | tf_op jit(solution)/shard_map/all_to_all | solution.py:187
  51.7 0.0 copy-done.4
  51.7 0.0 copy-done.1
  51.7 0.0 copy-done.3
  51.7 1.4 %shard_map.84 = (bf16[8,128,128]{2,1,0:T(8,128)(2,1)S(1)}, f32[128,1024]{1,0:T(8,128)S(1)}) custom-call(bf16[128,1024]{1,0:T(8,128)(2,1)S(1)} %copy-done.4, bf16[128,1024]{1,0:T(8,128)(2,1)S(1)} %copy-done.1, bf16[128,1024]{1,0:T(8,128)(2,1)S(1)} %copy-done.3), custom_call_target="tpu_custom_call" | custom-call | flops 67108864 | bytes 1572864 | tf_op jit(solution)/shard_map/pallas_call | solution.py:196
  53.1 0.0 copy-start.5
  53.1 5.8 %all-to-all-done.2 = bf16[16,32,128]{2,1,0:T(8,128)(2,1)S(1)} async-done(((bf16[16,32,128]{2,1,0:T(8,128)(2,1)}), bf16[16,32,128]{2,1,0:T(8,128)(2,1)S(1)}, u32[]{:S(2)}, u32[]{:S(2)}) %all-to-all-start.2) | async-done | bytes 131104 | tf_op jit(solution)/shard_map/all_to_all | solution.py:187
  58.9 0.0 copy-start.6
  58.9 6.9 %all_gather.20.chips_ref = bf16[1024,128]{1,0:T(8,128)(2,1)S(1)} all-gather(bf16[512,128]{1,0:T(8,128)(2,1)S(1)} %bitcast.37), channel_id=1, replica_groups=mesh['x'=4,'zh'=4,'zl'=4,'core'=2,'head'=4] {'core'}, dimensions={0}, use_global_device_ids=true | all-gather | bytes 393216 | tf_op jit(solution)/shard_map/all_gather | solution.py:188
  65.8 0.0 copy-done.5
  65.8 0.0 copy-done.6
  65.8 0.3 shard_map.89
  66.1 8.2 %all_to_all.80 = f32[4,8,128]{2,1,0:T(8,128)S(1)} all-to-all(f32[4,8,128]{2,1,0:T(8,128)S(1)} %bitcast.35), channel_id=1, replica_groups=mesh['x'=4,'zh'=4,'zl'=4,'core'=2,'head'=4] {'head'}, dimensions={0} | all-to-all | bytes 32768 | tf_op jit(solution)/shard_map/all_to_all | solution.py:205
  74.3 1.0 shard_map.90
  75.3 3.6 %all-gather.1 = bf16[16,128,128]{2,1,0:T(8,128)(2,1)S(1)} all-gather(bf16[8,128,128]{2,1,0:T(8,128)(2,1)S(1)} %get-tuple-element.33), channel_id=3, replica_groups=mesh['x'=4,'zh'=4,'zl'=4,'core'=2,'head'=4] {'core'}, dimensions={0}, use_global_device_ids=true | all-gather | bytes 786432 | tf_op jit(solution)/shard_map/all_gather | solution.py:211
  78.9 9.8 %all_to_all.81 = bf16[16,32,128]{2,1,0:T(8,128)(2,1)S(1)} all-to-all(bf16[16,32,128]{2,1,0:T(8,128)(2,1)S(1)} %bitcast.28), channel_id=1, replica_groups=mesh['x'=4,'zh'=4,'zl'=4,'core'=2,'head'=4] {'x','zl'}, dimensions={0} | all-to-all | bytes 262144 | tf_op jit(solution)/shard_map/all_to_all | solution.py:182
  88.8 15.9 %all_to_all.82 = bf16[4,128,128]{2,1,0:T(8,128)(2,1)S(1)} all-to-all(bf16[4,128,128]{2,1,0:T(8,128)(2,1)S(1)} %bitcast.31), channel_id=1, replica_groups=mesh['x'=4,'zh'=4,'zl'=4,'core'=2,'head'=4] {'zh'}, dimensions={0} | all-to-all | bytes 262144 | tf_op jit(solution)/shard_map/all_to_all | solution.py:184
  104.7 0.7 shard_map.94
  105.4 3.5 %all-to-all-start.6 = ((bf16[16,32,128]{2,1,0:T(8,128)(2,1)}), bf16[16,32,128]{2,1,0:T(8,128)(2,1)S(1)}, u32[]{:S(2)}, u32[]{:S(2)}) async-start(bf16[16,32,128]{2,1,0:T(8,128)(2,1)} %bitcast.17), calls=%async_computation.6 | async-start | bytes 262144 | tf_op jit(solution)/shard_map/all_to_all | solution.py:187
  108.9 2.1 %shard_map.91 = (bf16[128,1024]{1,0:T(8,128)(2,1)}, f32[128,1024]{1,0:T(8,128)S(1)}, f32[128,1024]{1,0:T(8,128)S(1)}) custom-call(bf16[128,1024]{1,0:T(8,128)(2,1)S(1)} %copy-done.4, bf16[128,1024]{1,0:T(8,128)(2,1)S(1)} %copy-done.1, bf16[128,1024]{1,0:T(8,128)(2,1)S(1)} %copy-done.3, bf16[128,1024]{1,0:T(8,128)(2,1)S(1)} %get-tuple-element.26.g_ref, ...), custom_call_target="tpu_custom_call" | custom-call | flops 167772160 | bytes 2883584 | tf_op jit(solution)/shard_map/pallas_call | solution.py:212
  111.0 5.1 %all-to-all-done.6 = bf16[16,32,128]{2,1,0:T(8,128)(2,1)S(1)} async-done(((bf16[16,32,128]{2,1,0:T(8,128)(2,1)}), bf16[16,32,128]{2,1,0:T(8,128)(2,1)S(1)}, u32[]{:S(2)}, u32[]{:S(2)}) %all-to-all-start.6) | async-done | bytes 131104 | tf_op jit(solution)/shard_map/all_to_all | solution.py:187
  116.1 6.6 %all_gather.23.chips_ref = bf16[1024,128]{1,0:T(8,128)(2,1)S(1)} all-gather(bf16[512,128]{1,0:T(8,128)(2,1)S(1)} %bitcast.36), channel_id=1, replica_groups=mesh['x'=4,'zh'=4,'zl'=4,'core'=2,'head'=4] {'core'}, dimensions={0}, use_global_device_ids=true | all-gather | bytes 393216 | tf_op jit(solution)/shard_map/all_gather | solution.py:188
  122.7 1.2 shard_map.95
  (3 shorter events, 0.1 us)
Async XLA Ops:
  0.6 1.0 copy-start
  1.6 0.9 copy-start.2
  22.1 29.6 %copy-start.4 = (bf16[128,1024]{1,0:T(8,128)(2,1)S(1)}, bf16[128,1024]{1,0:T(8,128)(2,1)}, u32[]{:S(2)}) copy-start(bf16[128,1024]{1,0:T(8,128)(2,1)} %q_ref.7) | copy-start | bytes 786436
  22.1 25.4 %all-to-all-start.1 = ((bf16[4,128,128]{2,1,0:T(8,128)(2,1)}), bf16[4,128,128]{2,1,0:T(8,128)(2,1)S(1)}, u32[]{:S(2)}, u32[]{:S(2)}) async-start(bf16[4,128,128]{2,1,0:T(8,128)(2,1)} %bitcast.5), calls=%async_computation.1 | async-start | bytes 262144 | tf_op jit(solution)/shard_map/all_to_all | solution.py:184
  47.4 4.2 %copy-start.1 = (bf16[128,1024]{1,0:T(8,128)(2,1)S(1)}, bf16[128,1024]{1,0:T(8,128)(2,1)}, u32[]{:S(2)}) copy-start(bf16[128,1024]{1,0:T(8,128)(2,1)} %k_ref.7) | copy-start | bytes 786436
  47.5 4.3 %copy-start.3 = (bf16[128,1024]{1,0:T(8,128)(2,1)S(1)}, bf16[128,1024]{1,0:T(8,128)(2,1)}, u32[]{:S(2)}) copy-start(bf16[128,1024]{1,0:T(8,128)(2,1)} %v_ref.7) | copy-start | bytes 786436
  48.2 10.7 %all-to-all-start.2 = ((bf16[16,32,128]{2,1,0:T(8,128)(2,1)}), bf16[16,32,128]{2,1,0:T(8,128)(2,1)S(1)}, u32[]{:S(2)}, u32[]{:S(2)}) async-start(bf16[16,32,128]{2,1,0:T(8,128)(2,1)} %bitcast.7), calls=%async_computation.2 | async-start | bytes 262144 | tf_op jit(solution)/shard_map/all_to_all | solution.py:187
  53.1 12.7 %copy-start.5 = (bf16[128,1024]{1,0:T(8,128)(2,1)S(1)}, bf16[128,1024]{1,0:T(8,128)(2,1)}, u32[]{:S(2)}) copy-start(bf16[128,1024]{1,0:T(8,128)(2,1)} %c_ref.3) | copy-start | bytes 786436
  58.9 6.9 %copy-start.6 = (f32[1024]{0:T(1024)S(1)}, f32[1024]{0:T(1024)}, u32[]{:S(2)}) copy-start(f32[1024]{0:T(1024)} %param.8) | copy-start | bytes 12292
  105.4 10.7 %all-to-all-start.6 = ((bf16[16,32,128]{2,1,0:T(8,128)(2,1)}), bf16[16,32,128]{2,1,0:T(8,128)(2,1)S(1)}, u32[]{:S(2)}, u32[]{:S(2)}) async-start(bf16[16,32,128]{2,1,0:T(8,128)(2,1)} %bitcast.17), calls=%async_computation.6 | async-start | bytes 262144 | tf_op jit(solution)/shard_map/all_to_all | solution.py:187

commit v3 on v2

v3 whole, which is shorter than its diff:
```python
import functools

import jax
import jax.numpy as jnp
from jax import lax
from jax.experimental import pallas as pl
from jax.experimental.pallas import tpu as pltpu
from jax.sharding import Mesh, PartitionSpec as P

HEADS = 32
DH = 128
ROWS = 128
X, ZH, ZL, CORES, GROUPS = 4, 4, 4, 2, 4
LOCAL = HEADS // GROUPS
HALF = LOCAL // CORES
CHUNK = CORES * ROWS
WIDTH = LOCAL * DH
PART = HALF * DH
WIDTH_ALL = HEADS * DH
EPSILON = 1e-06
PIECE = PART // (X * ZL)
X_ORDER = (2, 3, 0, 1)
ZL_ORDER = (3, 2, 1, 0)
ZH_ORDER = (2, 3, 0, 1)
PLANE = [[x * ZL + z for x in X_ORDER for z in ZL_ORDER]]
F32 = jnp.float32
BF16 = jnp.bfloat16

VMEM = pl.BlockSpec(memory_space=pltpu.VMEM)
SMEM = pl.BlockSpec(memory_space=pltpu.SMEM)


def dot(a, b, ca, cb):
    return lax.dot_general(a, b, (((ca,), (cb,)), ((), ())), preferred_element_type=F32)


def at(h):
    return slice(h * DH, (h + 1) * DH)


def wide(core_ref, ref, h):
    start = pl.multiple_of(core_ref[0] * PART, PART) + h * DH
    return ref[:, pl.ds(pl.multiple_of(start, DH), DH)]


def causal():
    t = lax.broadcasted_iota(jnp.int32, (CHUNK, CHUNK), 0)
    s = lax.broadcasted_iota(jnp.int32, (CHUNK, CHUNK), 1)
    return s <= t


def call(kernel, shapes, flops, moved, specs):
    return pl.pallas_call(
        kernel,
        out_shape=[jax.ShapeDtypeStruct(s, d) for s, d in shapes],
        in_specs=specs,
        out_specs=[VMEM] * len(shapes),
        compiler_params=pltpu.CompilerParams(vmem_limit_bytes=32 * 1024 * 1024),
        cost_estimate=pl.CostEstimate(flops=flops, bytes_accessed=moved, transcendentals=0),
    )


MATMUL = LOCAL * 2 * DH * DH * DH
BLOCK = ROWS * WIDTH * 2


def states_kernel(core_ref, k_ref, v_ref, mine_ref):
    for h in range(HALF):
        mine_ref[at(h), :] = dot(wide(core_ref, k_ref, h), wide(core_ref, v_ref, h), 0, 0).astype(BF16)


def spot(x, z):
    return (X_ORDER.index(x) * ZL + ZL_ORDER.index(z)) * PIECE


def piece(ref, start):
    return ref[start : start + PIECE, :].astype(F32)


def cube_kernel(in_ref, out_ref):
    for x in range(X):
        total = piece(in_ref, spot(x, 0))
        for z in range(1, ZL):
            total = total + piece(in_ref, spot(x, z))
        total = total.astype(BF16)
        for copy in range(ZH):
            start = (copy * X + x) * PIECE
            out_ref[start : start + PIECE, :] = total


def scan_kernel(reverse, place_ref, in_ref, cubes_ref, out_ref):
    here = place_ref[0]
    order = (lambda n: reversed(range(n))) if reverse else range
    column = jnp.zeros((PIECE, DH), F32)
    for x in order(X):
        total = column
        for z in range(ZH):
            cube = piece(cubes_ref, (ZH_ORDER.index(z) * X + x) * PIECE)
            column = column + cube
            ahead = here < z if reverse else here > z
            total = total + jnp.where(ahead, cube, 0.0)
        for z in order(ZL):
            start = spot(x, z)
            out_ref[start : start + PIECE, :] = total.astype(BF16)
            total = total + piece(in_ref, start)


def inside_kernel(core_ref, q_ref, k_ref, v_ref, scores_ref, inside_ref):
    mask = causal()
    for h in range(HALF):
        raw = dot(wide(core_ref, q_ref, h), wide(core_ref, k_ref, h), 1, 1)
        scores = jnp.where(mask, raw, 0.0).astype(BF16)
        scores_ref[h] = scores
        inside_ref[:, at(h)] = dot(scores, wide(core_ref, v_ref, h), 1, 0)


def rows_of(block):
    return [jnp.sum(block[i * ROWS : (i + 1) * ROWS].T, axis=0, keepdims=True) for i in range(CORES)]


def attended_kernel(core_ref, q_ref, inside_ref, before_ref, c_ref, gain_ref, att_ref, sums_ref):
    squares = jnp.zeros((CHUNK, DH), F32)
    crossed = jnp.zeros((CHUNK, DH), F32)
    for h in range(HALF):
        att = inside_ref[:, at(h)] + dot(wide(core_ref, q_ref, h), before_ref[at(h), :], 1, 0)
        att_ref[:, at(h)] = att
        weighted = wide(core_ref, c_ref, h).astype(F32) * wide(core_ref, gain_ref, h)
        squares = squares + att * att
        crossed = crossed + weighted * att
    block = jnp.concatenate(rows_of(squares) + rows_of(crossed) + [jnp.zeros((4, ROWS), F32)], axis=0)
    for i in range(CORES * GROUPS):
        sums_ref[i * 8 : (i + 1) * 8, :] = block


def tall(rows):
    return jnp.concatenate([jnp.broadcast_to(row, (ROWS, ROWS)).T for row in rows], axis=0)


def grad_kernel(core_ref, sums_ref, att_ref, q_ref, c_ref, gain_ref, normed_ref, g_ref, mine_ref):
    sums = sums_ref[0:8, :]
    for i in range(1, CORES * GROUPS):
        sums = sums + sums_ref[i * 8 : (i + 1) * 8, :]
    inverse_rows = lax.rsqrt(sums[0:2] / WIDTH_ALL + EPSILON)
    cubed_rows = inverse_rows * inverse_rows * inverse_rows * (sums[2:4] / WIDTH_ALL)
    inverse = tall([inverse_rows[0:1], inverse_rows[1:2]])
    cubed = tall([cubed_rows[0:1], cubed_rows[1:2]])
    for h in range(HALF):
        att = att_ref[:, at(h)]
        gain = wide(core_ref, gain_ref, h)
        normed_ref[:, at(h)] = (att * inverse * gain).astype(BF16)
        weighted = wide(core_ref, c_ref, h).astype(F32) * gain
        g = (inverse * weighted - cubed * att).astype(BF16)
        g_ref[:, at(h)] = g
        mine_ref[at(h), :] = dot(wide(core_ref, q_ref, h), g, 0, 0).astype(BF16)


def local_grads_kernel(core_ref, q_ref, k_ref, v_ref, g_ref, scores_ref, before_ref, gq_ref, gk_ref, gv_ref):
    mask = causal()
    for h in range(HALF):
        g = g_ref[:, at(h)]
        raw = dot(g, wide(core_ref, v_ref, h), 1, 1)
        grad_scores = jnp.where(mask, raw, 0.0).astype(BF16)
        gq = dot(grad_scores, wide(core_ref, k_ref, h), 1, 0) + dot(g, before_ref[at(h), :], 1, 1)
        gq_ref[:, at(h)] = gq.astype(BF16)
        gk_ref[:, at(h)] = dot(grad_scores, wide(core_ref, q_ref, h), 0, 0)
        gv_ref[:, at(h)] = dot(scores_ref[h], g, 0, 0)


def own_rows(core):
    return pl.ds(pl.multiple_of(core * ROWS, ROWS), ROWS)


def last_kernel(core_ref, k_ref, v_ref, gk_part_ref, gv_part_ref, beyond_ref, keep_ref, send_ref):
    core = core_ref[0]
    for h in range(HALF):
        column = pl.ds(pl.multiple_of(core * PART + h * DH, DH), DH)
        beyond = beyond_ref[at(h), :]
        for out_ref, rows in ((keep_ref, own_rows(core)), (send_ref, own_rows(1 - core))):
            gk = gk_part_ref[rows, at(h)] + dot(v_ref[rows, column], beyond, 1, 1)
            gv = gv_part_ref[rows, at(h)] + dot(k_ref[rows, column], beyond, 1, 0)
            out_ref[0:ROWS, at(h)] = gk.astype(BF16)
            out_ref[ROWS : 2 * ROWS, at(h)] = gv.astype(BF16)


def join_kernel(core_ref, keep_ref, got_ref, first_ref, second_ref):
    mine = pl.ds(pl.multiple_of(core_ref[0] * PART, PART), PART)
    other = pl.ds(pl.multiple_of((1 - core_ref[0]) * PART, PART), PART)
    for i, out_ref in enumerate((first_ref, second_ref)):
        rows = slice(i * ROWS, (i + 1) * ROWS)
        out_ref[:, mine] = keep_ref[rows, :]
        out_ref[:, other] = got_ref[rows, :]


def pick_kernel(core_ref, all_ref, out_ref):
    for i in range(CORES):
        rows = pl.ds(pl.multiple_of(i * CHUNK + core_ref[0] * ROWS, ROWS), ROWS)
        out_ref[:, i * PART : (i + 1) * PART] = all_ref[rows, :]


FLAT = (PART, DH)
TALL = (CHUNK, PART)
SCORES = (HALF, CHUNK, CHUNK)
OUT = (ROWS, WIDTH)


def plane_swap(a):
    return lax.all_to_all(a, ("x", "zl"), 0, 0, axis_index_groups=PLANE, tiled=True)


def chips_scan(mine, reverse, beside_turn=lambda: None, beside_cubes=lambda: None):
    place = lax.axis_index("zh").reshape(1).astype(jnp.int32)
    turned = plane_swap(mine)
    (cube,) = call(cube_kernel, [(FLAT, BF16)], 0, BLOCK, [VMEM])(turned)
    cube, extra = lax.optimization_barrier((cube, beside_turn()))
    cubes = lax.all_to_all(cube, "zh", 0, 0, axis_index_groups=[list(ZH_ORDER)], tiled=True)
    scan = functools.partial(scan_kernel, reverse)
    (summed,) = call(scan, [(FLAT, BF16)], 0, 2 * BLOCK, [SMEM, VMEM, VMEM])(place, turned, cubes)
    summed, more = lax.optimization_barrier((summed, beside_cubes()))
    return plane_swap(summed), extra, more


def pair(a):
    return lax.all_gather(a, "core", axis=0, tiled=True)


def picked(core, a):
    (out,) = call(pick_kernel, [(OUT, BF16)], 0, 3 * BLOCK, [SMEM, VMEM])(core, pair(a))
    return out


def local(q, k, v, gain, c):
    core = lax.axis_index("core").reshape(1).astype(jnp.int32)
    gain = gain.reshape(1, WIDTH)
    k, v, q, c = pair(k), pair(v), pair(q), pair(c)
    (mine,) = call(states_kernel, [(FLAT, BF16)], MATMUL, 5 * BLOCK, [SMEM] + [VMEM] * 2)(core, k, v)
    scores, inside = call(
        inside_kernel, [(SCORES, BF16), (TALL, F32)], 4 * MATMUL, 10 * BLOCK, [SMEM] + [VMEM] * 3
    )(core, q, k, v)
    before, _, _ = chips_scan(mine, False)
    att, sums = call(
        attended_kernel, [(TALL, F32), ((CORES * GROUPS * 8, ROWS), F32)], MATMUL, 10 * BLOCK, [SMEM] + [VMEM] * 5
    )(core, q, inside, before, c, gain)
    sums = lax.all_to_all(sums, ("core", "head"), 0, 0, tiled=True)
    normed, g, mine = call(
        grad_kernel, [(TALL, BF16), (TALL, BF16), (FLAT, BF16)], MATMUL, 9 * BLOCK, [SMEM] + [VMEM] * 5
    )(core, sums, att, q, c, gain)

    def grads():
        gq, gk_part, gv_part = call(
            local_grads_kernel, [(TALL, BF16), (TALL, F32), (TALL, F32)], 8 * MATMUL, 16 * BLOCK, [SMEM] + [VMEM] * 6
        )(core, q, k, v, g, scores, before)
        return picked(core, gq), gk_part, gv_part

    beyond, normed, (gq, gk_part, gv_part) = chips_scan(mine, True, lambda: picked(core, normed), grads)
    keep, send = call(last_kernel, [(TALL, BF16), (TALL, BF16)], 2 * MATMUL, 11 * BLOCK, [SMEM] + [VMEM] * 5)(
        core, k, v, gk_part, gv_part, beyond
    )
    got = lax.ppermute(send, "core", [(0, 1), (1, 0)])
    gk, gv = call(join_kernel, [(OUT, BF16), (OUT, BF16)], 0, 4 * BLOCK, [SMEM, VMEM, VMEM])(core, keep, got)
    return normed, gq, gk, gv


def solution(mesh):
    fine = Mesh(mesh.devices.reshape(X, ZH, ZL, CORES, GROUPS), ("x", "zh", "zl", "core", "head"))
    block = P(("x", "zh", "zl", "core"), "head")
    return jax.shard_map(
        local, mesh=fine, in_specs=(block, block, block, P("head"), block), out_specs=(block,) * 4, check_vma=False
    )
```

time: 125 us -> 117 us (0.936)
  starting transfers between devices: 19.3 us -> 43.3 us
  waiting for transfers between devices: 24.1 us -> 6.32 us
  blocking collectives: 69.6 us -> 54.8 us
    all_to_all x3 -> x4, starting transfers between devices: 19.3 us -> 38.4 us  [the longest x2 24.1 us: chips_scan(): lax.all_to_all(cube, 'zh', 0, 0, axis_index_groups=[list(ZH_ORDER)], tile...]
    all_to_all x3 -> x4, waiting for transfers between devices: 24.1 us -> 5.18 us  [the longest x2 4.84 us: chips_scan(): lax.all_to_all(cube, 'zh', 0, 0, axis_index_groups=[list(ZH_ORDER)], tile...]
    all_to_all x4 -> x3, blocking collectives: 43.8 us -> 30.2 us  [the longest x2 20.6 us: plane_swap(): lax.all_to_all(a, ('x', 'zl'), 0, 0, axis_index_groups=PLANE, tiled=True)]
    ppermute x0 -> x1, starting transfers between devices: none -> 4.84 us  [local(): got = lax.ppermute(send, 'core', [(0, 1), (1, 0)])]
    all_gather x4 -> x6, blocking collectives: 25.7 us -> 24.6 us  [pair(): return lax.all_gather(a, 'core', axis=0, tiled=True)]
    unnamed x14 -> x12, local copies, waits for them, and re-layouts: 1.92 us -> 2.52 us
    pallas_call x8 -> x9, Pallas kernels: 6.21 us -> 6.42 us  [the longest x2 1.44 us: picked(): call(pick_kernel, [(OUT, BF16)], 0, 3 * BLOCK, [SMEM, VMEM])(core, pair(a))]
  transfers between devices with their start and end apart: 3 -> 5, of which waited for: 3 -> 3; matrix products, arithmetic and copies ran while one was open for 0% -> 0% of each run, Pallas kernels for 3% -> 3%
where the time goes in v3:
time: 117 us; the launch traced here: 116 us
  blocking collectives  54.8 us (47%)
  starting transfers between devices  43.3 us (37%)
  Pallas kernels  8.52 us (7%)
  waiting for transfers between devices  6.32 us (5%)
  local copies, waits for them, and re-layouts  2.52 us (2%)
    all_gather x6, blocking collectives, pair(): return lax.all_gather(a, 'core', axis=0, tiled=True)  24.6 us
    all_to_all x2, starting transfers between devices, chips_scan(): lax.all_to_all(cube, 'zh', 0, 0, axis_index_groups=[list(ZH_ORDER)], tile...  24.1 us
    all_to_all x2, blocking collectives, plane_swap(): lax.all_to_all(a, ('x', 'zl'), 0, 0, axis_index_groups=PLANE, tiled=True)  20.6 us
    all_to_all x2, starting transfers between devices, plane_swap(): lax.all_to_all(a, ('x', 'zl'), 0, 0, axis_index_groups=PLANE, tiled=True)  14.4 us
    all_to_all x1, blocking collectives, local(): sums = lax.all_to_all(sums, ('core', 'head'), 0, 0, tiled=True)  9.56 us
    all_to_all x2, waiting for transfers between devices, chips_scan(): lax.all_to_all(cube, 'zh', 0, 0, axis_index_groups=[list(ZH_ORDER)], tile...  4.84 us
    ppermute x1, starting transfers between devices, local(): got = lax.ppermute(send, 'core', [(0, 1), (1, 0)])  4.84 us
    unnamed x12, local copies, waits for them, and re-layouts  2.52 us
  transfers between devices with their start and end apart: 5, of which 3 were waited for; matrix products, arithmetic and copies ran while one was open for 0% of the time, Pallas kernels for 3%

profile of v3, /device:TPU:1, one launch (start us, length us, event | category | flops | bytes accessed | tf_op | source)
XLA Modules:
  0.0 116.1 jit_solution(10568841723077691301)
XLA Ops:
  0.6 0.0 copy-start.3
  0.6 9.0 %all_gather.19.k_ref = bf16[256,1024]{1,0:T(8,128)(2,1)S(1)} all-gather(bf16[128,1024]{1,0:T(8,128)(2,1)} %param.6), channel_id=1, replica_groups=mesh['x'=4,'zh'=4,'zl'=4,'core'=2,'head'=4] {'core'}, dimensions={0}, use_global_device_ids=true | all-gather | bytes 786432 | tf_op jit(solution)/shard_map/all_gather | solution.py:223
  9.7 0.0 copy-done.3
  9.7 2.2 %all_gather.20.v_ref = bf16[256,1024]{1,0:T(8,128)(2,1)S(1)} all-gather(bf16[128,1024]{1,0:T(8,128)(2,1)S(1)} %copy-done.3), channel_id=1, replica_groups=mesh['x'=4,'zh'=4,'zl'=4,'core'=2,'head'=4] {'core'}, dimensions={0}, use_global_device_ids=true | all-gather | bytes 786432 | tf_op jit(solution)/shard_map/all_gather | solution.py:223
  11.8 0.3 shard_map.85
  12.2 10.6 %all_to_all.77 = bf16[16,32,128]{2,1,0:T(8,128)(2,1)S(1)} all-to-all(bf16[16,32,128]{2,1,0:T(8,128)(2,1)S(1)} %bitcast.24), channel_id=1, replica_groups={{280,272,264,256,408,400,392,384,24,16,8,0,152,144,136,128},{281,273,26..., dimensions={0} | all-to-all | bytes 262144 | tf_op jit(solution)/shard_map/all_to_all | solution.py:207
  22.7 0.7 shard_map.86
  23.4 12.2 %all-to-all-start.1 = ((bf16[4,128,128]{2,1,0:T(8,128)(2,1)}), bf16[4,128,128]{2,1,0:T(8,128)(2,1)S(1)}, u32[]{:S(2)}, u32[]{:S(2)}) async-start(bf16[4,128,128]{2,1,0:T(8,128)(2,1)} %bitcast.4), calls=%async_computation.1 | async-start | bytes 262144 | tf_op jit(solution)/shard_map/all_to_all | solution.py:215
  35.6 4.8 %all-to-all-done.1 = bf16[4,128,128]{2,1,0:T(8,128)(2,1)S(1)} async-done(((bf16[4,128,128]{2,1,0:T(8,128)(2,1)}), bf16[4,128,128]{2,1,0:T(8,128)(2,1)S(1)}, u32[]{:S(2)}, u32[]{:S(2)}) %all-to-all-start.1) | async-done | bytes 131104 | tf_op jit(solution)/shard_map/all_to_all | solution.py:215
  40.5 0.0 copy-start.4
  40.5 0.7 shard_map.87
  41.2 7.4 %all-to-all-start.2 = ((bf16[16,32,128]{2,1,0:T(8,128)(2,1)}), bf16[16,32,128]{2,1,0:T(8,128)(2,1)S(1)}, u32[]{:S(2)}, u32[]{:S(2)}) async-start(bf16[16,32,128]{2,1,0:T(8,128)(2,1)} %bitcast.6), calls=%async_computation.2 | async-start | bytes 262144 | tf_op jit(solution)/shard_map/all_to_all | solution.py:207
  48.6 0.0 copy-done.4
  48.6 5.3 %all_gather.18.q_ref = bf16[256,1024]{1,0:T(8,128)(2,1)S(1)} all-gather(bf16[128,1024]{1,0:T(8,128)(2,1)S(1)} %copy-done.4), channel_id=1, replica_groups=mesh['x'=4,'zh'=4,'zl'=4,'core'=2,'head'=4] {'core'}, dimensions={0}, use_global_device_ids=true | all-gather | bytes 786432 | tf_op jit(solution)/shard_map/all_gather | solution.py:223
  53.9 0.0 copy-start.5
  53.9 0.7 shard_map.84
  54.5 0.0 copy-start
  54.6 0.8 copy-done
  55.3 0.0 copy-done.5
  55.3 2.2 %all_gather.21.c_ref = bf16[256,1024]{1,0:T(8,128)(2,1)S(1)} all-gather(bf16[128,1024]{1,0:T(8,128)(2,1)S(1)} %copy-done.5), channel_id=1, replica_groups=mesh['x'=4,'zh'=4,'zl'=4,'core'=2,'head'=4] {'core'}, dimensions={0}, use_global_device_ids=true | all-gather | bytes 786432 | tf_op jit(solution)/shard_map/all_gather | solution.py:223
  57.5 0.0 copy-start.2
  57.5 0.0 all-to-all-done.2
  57.5 0.7 copy-done.2
  58.2 0.4 shard_map.88
  58.6 9.6 %all_to_all.78 = f32[8,8,128]{2,1,0:T(8,128)S(1)} all-to-all(f32[8,8,128]{2,1,0:T(8,128)S(1)} %bitcast.29), channel_id=1, replica_groups=mesh['x'=4,'zh'=4,'zl'=4,'core'=2,'head'=4] {'core','head'}, dimensions={0} | all-to-all | bytes 65536 | tf_op jit(solution)/shard_map/all_to_all | solution.py:243
  68.1 1.1 shard_map.89
  69.2 7.0 %all-to-all-start.4 = ((bf16[16,32,128]{2,1,0:T(8,128)(2,1)}), bf16[16,32,128]{2,1,0:T(8,128)(2,1)S(1)}, u32[]{:S(2)}, u32[]{:S(2)}) async-start(bf16[16,32,128]{2,1,0:T(8,128)(2,1)} %bitcast.11), calls=%async_computation.4 | async-start | bytes 262144 | tf_op jit(solution)/shard_map/all_to_all | solution.py:207
  76.2 2.7 %all_gather.22.all_ref = bf16[512,512]{1,0:T(8,128)(2,1)S(1)} all-gather(bf16[256,512]{1,0:T(8,128)(2,1)S(1)} %get-tuple-element.28), channel_id=1, replica_groups=mesh['x'=4,'zh'=4,'zl'=4,'core'=2,'head'=4] {'core'}, dimensions={0}, use_global_device_ids=true | all-gather | bytes 786432 | tf_op jit(solution)/shard_map/all_gather | solution.py:223
  79.0 0.7 shard_map.91
  79.7 0.3 all-to-all-done.4
  80.0 0.7 shard_map.90
  80.7 11.8 %all-to-all-start.5 = ((bf16[4,128,128]{2,1,0:T(8,128)(2,1)}), bf16[4,128,128]{2,1,0:T(8,128)(2,1)S(1)}, u32[]{:S(2)}, u32[]{:S(2)}) async-start(bf16[4,128,128]{2,1,0:T(8,128)(2,1)} %bitcast.13), calls=%async_computation.5 | async-start | bytes 262144 | tf_op jit(solution)/shard_map/all_to_all | solution.py:215
  92.5 0.0 copy-start.1
  92.5 1.0 copy-done.1
  93.6 1.3 %shard_map.93 = (bf16[256,512]{1,0:T(8,128)(2,1)S(1)}, f32[256,512]{1,0:T(8,128)S(1)}, f32[256,512]{1,0:T(8,128)S(1)}) custom-call(s32[1]{0:T(128)} %bitcast.core_ref, bf16[256,1024]{1,0:T(8,128)(2,1)S(1)} %all_gather.18.q_ref, bf16[256,1024]{1,0:T(8,128)(2,1)S(1)} %all_gather.19.k_ref, bf16[256,1024]{1,0:T(8,128)(2,1)S(1)} %all_gather.20.v_ref, ...), custom_call_target="tpu_custom_call" | custom-call | flops 268435456 | bytes 4194304 | tf_op jit(solution)/shard_map/pallas_call | solution.py:249
  94.9 3.2 %all_gather.23.all_ref = bf16[512,512]{1,0:T(8,128)(2,1)S(1)} all-gather(bf16[256,512]{1,0:T(8,128)(2,1)S(1)} %get-tuple-element.33), channel_id=1, replica_groups=mesh['x'=4,'zh'=4,'zl'=4,'core'=2,'head'=4] {'core'}, dimensions={0}, use_global_device_ids=true | all-gather | bytes 786432 | tf_op jit(solution)/shard_map/all_gather | solution.py:223
  98.1 0.7 shard_map.94
  98.8 0.0 all-to-all-done.5
  98.8 0.1 shard_map.92
  98.9 10.0 %all_to_all.79 = bf16[16,32,128]{2,1,0:T(8,128)(2,1)S(1)} all-to-all(bf16[16,32,128]{2,1,0:T(8,128)(2,1)S(1)} %bitcast.27), channel_id=1, replica_groups={{280,272,264,256,408,400,392,384,24,16,8,0,152,144,136,128},{281,273,26..., dimensions={0} | all-to-all | bytes 262144 | tf_op jit(solution)/shard_map/all_to_all | solution.py:207
  108.9 0.4 shard_map.95
  109.3 4.8 %collective-permute-start = (bf16[256,512]{1,0:T(8,128)(2,1)S(1)}, bf16[256,512]{1,0:T(8,128)(2,1)S(1)}, u32[]{:S(2)}, u32[]{:S(2)}) collective-permute-start(bf16[256,512]{1,0:T(8,128)(2,1)S(1)} %get-tuple-element.41), channel_id=1, source_target_pairs={{0,4},{4,0},{1,5},{5,1},{2,6},{6,2},{3,7},{7,3},{8,12},{12,8},{9,1... | collective-permute-start | bytes 786440 | tf_op jit(solution)/shard_map/ppermute | solution.py:258
  114.2 1.1 collective-permute-done.got_ref
  115.3 0.8 shard_map.96
Async XLA Ops:
  0.6 9.0 %copy-start.3 = (bf16[128,1024]{1,0:T(8,128)(2,1)S(1)}, bf16[128,1024]{1,0:T(8,128)(2,1)}, u32[]{:S(2)}) copy-start(bf16[128,1024]{1,0:T(8,128)(2,1)} %param.7) | copy-start | bytes 786436
  23.4 17.1 %all-to-all-start.1 = ((bf16[4,128,128]{2,1,0:T(8,128)(2,1)}), bf16[4,128,128]{2,1,0:T(8,128)(2,1)S(1)}, u32[]{:S(2)}, u32[]{:S(2)}) async-start(bf16[4,128,128]{2,1,0:T(8,128)(2,1)} %bitcast.4), calls=%async_computation.1 | async-start | bytes 262144 | tf_op jit(solution)/shard_map/all_to_all | solution.py:215
  40.5 8.1 %copy-start.4 = (bf16[128,1024]{1,0:T(8,128)(2,1)S(1)}, bf16[128,1024]{1,0:T(8,128)(2,1)}, u32[]{:S(2)}) copy-start(bf16[128,1024]{1,0:T(8,128)(2,1)} %param.5) | copy-start | bytes 786436
  41.2 16.3 %all-to-all-start.2 = ((bf16[16,32,128]{2,1,0:T(8,128)(2,1)}), bf16[16,32,128]{2,1,0:T(8,128)(2,1)S(1)}, u32[]{:S(2)}, u32[]{:S(2)}) async-start(bf16[16,32,128]{2,1,0:T(8,128)(2,1)} %bitcast.6), calls=%async_computation.2 | async-start | bytes 262144 | tf_op jit(solution)/shard_map/all_to_all | solution.py:207
  53.9 1.5 %copy-start.5 = (bf16[128,1024]{1,0:T(8,128)(2,1)S(1)}, bf16[128,1024]{1,0:T(8,128)(2,1)}, u32[]{:S(2)}) copy-start(bf16[128,1024]{1,0:T(8,128)(2,1)} %param.9) | copy-start | bytes 786436
  54.5 0.8 copy-start
  57.5 0.7 copy-start.2
  69.2 10.8 %all-to-all-start.4 = ((bf16[16,32,128]{2,1,0:T(8,128)(2,1)}), bf16[16,32,128]{2,1,0:T(8,128)(2,1)S(1)}, u32[]{:S(2)}, u32[]{:S(2)}) async-start(bf16[16,32,128]{2,1,0:T(8,128)(2,1)} %bitcast.11), calls=%async_computation.4 | async-start | bytes 262144 | tf_op jit(solution)/shard_map/all_to_all | solution.py:207
  80.7 18.2 %all-to-all-start.5 = ((bf16[4,128,128]{2,1,0:T(8,128)(2,1)}), bf16[4,128,128]{2,1,0:T(8,128)(2,1)S(1)}, u32[]{:S(2)}, u32[]{:S(2)}) async-start(bf16[4,128,128]{2,1,0:T(8,128)(2,1)} %bitcast.13), calls=%async_computation.5 | async-start | bytes 262144 | tf_op jit(solution)/shard_map/all_to_all | solution.py:215
  92.5 1.0 copy-start.1
  109.3 6.0 %collective-permute-start = (bf16[256,512]{1,0:T(8,128)(2,1)S(1)}, bf16[256,512]{1,0:T(8,128)(2,1)S(1)}, u32[]{:S(2)}, u32[]{:S(2)}) collective-permute-start(bf16[256,512]{1,0:T(8,128)(2,1)S(1)} %get-tuple-element.41), channel_id=1, source_target_pairs={{0,4},{4,0},{1,5},{5,1},{2,6},{6,2},{3,7},{7,3},{8,12},{12,8},{9,1... | collective-permute-start | bytes 786440 | tf_op jit(solution)/shard_map/ppermute | solution.py:258

commit v4 on v3

--- a/solution.py
+++ b/solution.py
@@ -20,8 +20,8 @@
 EPSILON = 1e-06
 PIECE = PART // (X * ZL)
 X_ORDER = (2, 3, 0, 1)
-ZL_ORDER = (3, 2, 1, 0)
-ZH_ORDER = (2, 3, 0, 1)
+ZL_ORDER = (2, 1, 3, 0)
+ZH_ORDER = (2, 1, 3, 0)
 PLANE = [[x * ZL + z for x in X_ORDER for z in ZL_ORDER]]
 F32 = jnp.float32
 BF16 = jnp.bfloat16
@@ -105,28 +105,29 @@
             total = total + piece(in_ref, start)
 
 
-def inside_kernel(core_ref, q_ref, k_ref, v_ref, scores_ref, inside_ref):
+def inside_kernel(core_ref, q_ref, k_ref, v_ref, c_ref, gain_ref, inside_ref, weighted_ref, near_gain_ref):
     mask = causal()
     for h in range(HALF):
         raw = dot(wide(core_ref, q_ref, h), wide(core_ref, k_ref, h), 1, 1)
         scores = jnp.where(mask, raw, 0.0).astype(BF16)
-        scores_ref[h] = scores
         inside_ref[:, at(h)] = dot(scores, wide(core_ref, v_ref, h), 1, 0)
+        gain = wide(core_ref, gain_ref, h)
+        near_gain_ref[:, at(h)] = jnp.broadcast_to(gain, (8, DH))
+        weighted_ref[:, at(h)] = wide(core_ref, c_ref, h).astype(F32) * gain
 
 
 def rows_of(block):
     return [jnp.sum(block[i * ROWS : (i + 1) * ROWS].T, axis=0, keepdims=True) for i in range(CORES)]
 
 
-def attended_kernel(core_ref, q_ref, inside_ref, before_ref, c_ref, gain_ref, att_ref, sums_ref):
+def attended_kernel(core_ref, q_ref, inside_ref, before_ref, weighted_ref, att_ref, sums_ref):
     squares = jnp.zeros((CHUNK, DH), F32)
     crossed = jnp.zeros((CHUNK, DH), F32)
     for h in range(HALF):
         att = inside_ref[:, at(h)] + dot(wide(core_ref, q_ref, h), before_ref[at(h), :], 1, 0)
         att_ref[:, at(h)] = att
-        weighted = wide(core_ref, c_ref, h).astype(F32) * wide(core_ref, gain_ref, h)
         squares = squares + att * att
-        crossed = crossed + weighted * att
+        crossed = crossed + weighted_ref[:, at(h)] * att
     block = jnp.concatenate(rows_of(squares) + rows_of(crossed) + [jnp.zeros((4, ROWS), F32)], axis=0)
     for i in range(CORES * GROUPS):
         sums_ref[i * 8 : (i + 1) * 8, :] = block
@@ -136,7 +137,7 @@
     return jnp.concatenate([jnp.broadcast_to(row, (ROWS, ROWS)).T for row in rows], axis=0)
 
 
-def grad_kernel(core_ref, sums_ref, att_ref, q_ref, c_ref, gain_ref, normed_ref, g_ref, mine_ref):
+def grad_kernel(core_ref, sums_ref, att_ref, q_ref, weighted_ref, gain_ref, normed_ref, g_ref, mine_ref):
     sums = sums_ref[0:8, :]
     for i in range(1, CORES * GROUPS):
         sums = sums + sums_ref[i * 8 : (i + 1) * 8, :]
@@ -146,28 +147,30 @@
     cubed = tall([cubed_rows[0:1], cubed_rows[1:2]])
     for h in range(HALF):
         att = att_ref[:, at(h)]
-        gain = wide(core_ref, gain_ref, h)
-        normed_ref[:, at(h)] = (att * inverse * gain).astype(BF16)
-        weighted = wide(core_ref, c_ref, h).astype(F32) * gain
-        g = (inverse * weighted - cubed * att).astype(BF16)
+        normed_ref[:, at(h)] = (att * inverse * gain_ref[0:1, at(h)]).astype(BF16)
+        g = (inverse * weighted_ref[:, at(h)] - cubed * att).astype(BF16)
         g_ref[:, at(h)] = g
         mine_ref[at(h), :] = dot(wide(core_ref, q_ref, h), g, 0, 0).astype(BF16)
 
 
-def local_grads_kernel(core_ref, q_ref, k_ref, v_ref, g_ref, scores_ref, before_ref, gq_ref, gk_ref, gv_ref):
-    mask = causal()
-    for h in range(HALF):
-        g = g_ref[:, at(h)]
-        raw = dot(g, wide(core_ref, v_ref, h), 1, 1)
-        grad_scores = jnp.where(mask, raw, 0.0).astype(BF16)
-        gq = dot(grad_scores, wide(core_ref, k_ref, h), 1, 0) + dot(g, before_ref[at(h), :], 1, 1)
-        gq_ref[:, at(h)] = gq.astype(BF16)
-        gk_ref[:, at(h)] = dot(grad_scores, wide(core_ref, q_ref, h), 0, 0)
-        gv_ref[:, at(h)] = dot(scores_ref[h], g, 0, 0)
-
-
 def own_rows(core):
     return pl.ds(pl.multiple_of(core * ROWS, ROWS), ROWS)
+
+
+def local_grads_kernel(
+    core_ref, q_ref, k_ref, v_ref, g_ref, before_ref, normed_ref, keep_ref, send_ref, gk_ref, gv_ref, gq_ref
+):
+    mask = causal()
+    for h in range(HALF):
+        q, k, v, g = wide(core_ref, q_ref, h), wide(core_ref, k_ref, h), wide(core_ref, v_ref, h), g_ref[:, at(h)]
+        scores = jnp.where(mask, dot(q, k, 1, 1), 0.0).astype(BF16)
+        grad_scores = jnp.where(mask, dot(g, v, 1, 1), 0.0).astype(BF16)
+        gq_ref[:, at(h)] = (dot(grad_scores, k, 1, 0) + dot(g, before_ref[at(h), :], 1, 1)).astype(BF16)
+        gk_ref[:, at(h)] = dot(grad_scores, q, 0, 0)
+        gv_ref[:, at(h)] = dot(scores, g, 0, 0)
+    for out_ref, rows in ((keep_ref, own_rows(core_ref[0])), (send_ref, own_rows(1 - core_ref[0]))):
+        out_ref[0:ROWS, :] = normed_ref[rows, :]
+        out_ref[ROWS : 2 * ROWS, :] = gq_ref[rows, :]
 
 
 def last_kernel(core_ref, k_ref, v_ref, gk_part_ref, gv_part_ref, beyond_ref, keep_ref, send_ref):
@@ -182,24 +185,16 @@
             out_ref[ROWS : 2 * ROWS, at(h)] = gv.astype(BF16)
 
 
-def join_kernel(core_ref, keep_ref, got_ref, first_ref, second_ref):
-    mine = pl.ds(pl.multiple_of(core_ref[0] * PART, PART), PART)
-    other = pl.ds(pl.multiple_of((1 - core_ref[0]) * PART, PART), PART)
+def join_kernel(core_ref, keep_ref, sent_ref, first_ref, second_ref):
+    core, other = core_ref[0], 1 - core_ref[0]
     for i, out_ref in enumerate((first_ref, second_ref)):
-        rows = slice(i * ROWS, (i + 1) * ROWS)
-        out_ref[:, mine] = keep_ref[rows, :]
-        out_ref[:, other] = got_ref[rows, :]
-
-
-def pick_kernel(core_ref, all_ref, out_ref):
-    for i in range(CORES):
-        rows = pl.ds(pl.multiple_of(i * CHUNK + core_ref[0] * ROWS, ROWS), ROWS)
-        out_ref[:, i * PART : (i + 1) * PART] = all_ref[rows, :]
+        out_ref[:, pl.ds(pl.multiple_of(core * PART, PART), PART)] = keep_ref[i * ROWS : (i + 1) * ROWS, :]
+        rows = pl.ds(pl.multiple_of(other * CHUNK + i * ROWS, ROWS), ROWS)
+        out_ref[:, pl.ds(pl.multiple_of(other * PART, PART), PART)] = sent_ref[rows, :]
 
 
 FLAT = (PART, DH)
 TALL = (CHUNK, PART)
-SCORES = (HALF, CHUNK, CHUNK)
 OUT = (ROWS, WIDTH)
 
 
@@ -223,40 +218,42 @@
     return lax.all_gather(a, "core", axis=0, tiled=True)
 
 
-def picked(core, a):
-    (out,) = call(pick_kernel, [(OUT, BF16)], 0, 3 * BLOCK, [SMEM, VMEM])(core, pair(a))
-    return out
+def joined(core, keep, send):
+    return call(join_kernel, [(OUT, BF16), (OUT, BF16)], 0, 4 * BLOCK, [SMEM, VMEM, VMEM])(core, keep, pair(send))
 
 
 def local(q, k, v, gain, c):
     core = lax.axis_index("core").reshape(1).astype(jnp.int32)
     gain = gain.reshape(1, WIDTH)
-    k, v, q, c = pair(k), pair(v), pair(q), pair(c)
+    k, v = pair(k), pair(v)
     (mine,) = call(states_kernel, [(FLAT, BF16)], MATMUL, 5 * BLOCK, [SMEM] + [VMEM] * 2)(core, k, v)
-    scores, inside = call(
-        inside_kernel, [(SCORES, BF16), (TALL, F32)], 4 * MATMUL, 10 * BLOCK, [SMEM] + [VMEM] * 3
-    )(core, q, k, v)
-    before, _, _ = chips_scan(mine, False)
+    q, c = pair(q), pair(c)
+
+    def prepare():
+        return call(
+            inside_kernel, [(TALL, F32), (TALL, F32), ((8, PART), F32)], 4 * MATMUL, 12 * BLOCK, [SMEM] + [VMEM] * 5
+        )(core, q, k, v, c, gain)
+
+    before, q, (inside, weighted, near_gain) = chips_scan(mine, False, lambda: q, prepare)
     att, sums = call(
-        attended_kernel, [(TALL, F32), ((CORES * GROUPS * 8, ROWS), F32)], MATMUL, 10 * BLOCK, [SMEM] + [VMEM] * 5
-    )(core, q, inside, before, c, gain)
-    sums = lax.all_to_all(sums, ("core", "head"), 0, 0, tiled=True)
+        attended_kernel, [(TALL, F32), ((CORES * GROUPS * 8, ROWS), F32)], MATMUL, 10 * BLOCK, [SMEM] + [VMEM] * 4
+    )(core, q, inside, before, weighted)
+    sums = lax.all_to_all(sums, ("core", "head"), 0, 0, axis_index_groups=[[2, 6, 3, 7, 0, 4, 1, 5]], tiled=True)
     normed, g, mine = call(
         grad_kernel, [(TALL, BF16), (TALL, BF16), (FLAT, BF16)], MATMUL, 9 * BLOCK, [SMEM] + [VMEM] * 5
-    )(core, sums, att, q, c, gain)
-
-    def grads():
-        gq, gk_part, gv_part = call(
-            local_grads_kernel, [(TALL, BF16), (TALL, F32), (TALL, F32)], 8 * MATMUL, 16 * BLOCK, [SMEM] + [VMEM] * 6
-        )(core, q, k, v, g, scores, before)
-        return picked(core, gq), gk_part, gv_part
-
-    beyond, normed, (gq, gk_part, gv_part) = chips_scan(mine, True, lambda: picked(core, normed), grads)
+    )(core, sums, att, q, weighted, near_gain)
+    keep, send, gk_part, gv_part, _ = call(
+        local_grads_kernel,
+        [(TALL, BF16), (TALL, BF16), (TALL, F32), (TALL, F32), (TALL, BF16)],
+        12 * MATMUL, 18 * BLOCK, [SMEM] + [VMEM] * 6,
+    )(core, q, k, v, g, before, normed)
+    beyond, (gk_part, gv_part), (normed, gq) = chips_scan(
+        mine, True, lambda: (gk_part, gv_part), lambda: joined(core, keep, send)
+    )
     keep, send = call(last_kernel, [(TALL, BF16), (TALL, BF16)], 2 * MATMUL, 11 * BLOCK, [SMEM] + [VMEM] * 5)(
         core, k, v, gk_part, gv_part, beyond
     )
-    got = lax.ppermute(send, "core", [(0, 1), (1, 0)])
-    gk, gv = call(join_kernel, [(OUT, BF16), (OUT, BF16)], 0, 4 * BLOCK, [SMEM, VMEM, VMEM])(core, keep, got)
+    gk, gv = joined(core, keep, send)
     return normed, gq, gk, gv
 
 

time: 117 us -> 108 us (0.923)
  starting transfers between devices: 43.3 us -> 36.9 us
  waiting for transfers between devices: 6.32 us -> 0.4 us
  blocking collectives: 54.8 us -> 58.4 us
    ppermute x1 -> x0, starting transfers between devices: 4.84 us -> none  [local(): got = lax.ppermute(send, 'core', [(0, 1), (1, 0)])]
    all_to_all x2, waiting for transfers between devices: 4.84 us -> 0.01 us  [chips_scan(): lax.all_to_all(cube, 'zh', 0, 0, axis_index_groups=[list(ZH_ORDER)], tile...]
    all_gather x6, blocking collectives: 24.6 us -> 27.2 us  [pair(): return lax.all_gather(a, 'core', axis=0, tiled=True)]
    all_to_all x2, starting transfers between devices: 14.4 us -> 13 us  [plane_swap(): lax.all_to_all(a, ('x', 'zl'), 0, 0, axis_index_groups=PLANE, tiled=True)]
    all_to_all x1, blocking collectives: 9.56 us -> 10.8 us  [local(): lax.all_to_all(sums, ('core', 'head'), 0, 0, axis_index_groups=[[2, 6, 3,...]
    pallas_call x5 -> x4, Pallas kernels: 4.26 us -> 4.41 us  [the longest x1 2.08 us: local(): call(local_grads_kernel, [(TALL, BF16), (TALL, BF16), (TALL, F32), (TALL,...]
    unnamed x12 -> x16, local copies, waits for them, and re-layouts: 2.52 us -> 2.37 us
  transfers between devices with their start and end apart: 5 -> 4, of which waited for: 3 -> 1; matrix products, arithmetic and copies ran while one was open for 0% -> 0% of each run, Pallas kernels for 3% -> 3%
where the time goes in v4:
time: 108 us; the launch traced here: 107 us
  blocking collectives  58.4 us (54%)
  starting transfers between devices  36.9 us (34%)
  Pallas kernels  8.66 us (8%)
  local copies, waits for them, and re-layouts  2.37 us (2%)
    all_gather x6, blocking collectives, pair(): return lax.all_gather(a, 'core', axis=0, tiled=True)  27.2 us
    all_to_all x2, starting transfers between devices, chips_scan(): lax.all_to_all(cube, 'zh', 0, 0, axis_index_groups=[list(ZH_ORDER)], tile...  23.9 us
    all_to_all x2, blocking collectives, plane_swap(): lax.all_to_all(a, ('x', 'zl'), 0, 0, axis_index_groups=PLANE, tiled=True)  20.3 us
    all_to_all x2, starting transfers between devices, plane_swap(): lax.all_to_all(a, ('x', 'zl'), 0, 0, axis_index_groups=PLANE, tiled=True)  13 us
    all_to_all x1, blocking collectives, local(): lax.all_to_all(sums, ('core', 'head'), 0, 0, axis_index_groups=[[2, 6, 3,...  10.8 us
    unnamed x16, local copies, waits for them, and re-layouts  2.37 us
  transfers between devices with their start and end apart: 4, of which 1 were waited for; matrix products, arithmetic and copies ran while one was open for 0% of the time, Pallas kernels for 3%

profile of v4, /device:TPU:1, one launch (start us, length us, event | category | flops | bytes accessed | tf_op | source)
XLA Modules:
  0.0 107.4 jit_solution(10427942075517862630)
XLA Ops:
  0.6 0.0 copy-start.5
  0.6 9.0 %all_gather.18.k_ref = bf16[256,1024]{1,0:T(8,128)(2,1)S(1)} all-gather(bf16[128,1024]{1,0:T(8,128)(2,1)} %param.6), channel_id=1, replica_groups=mesh['x'=4,'zh'=4,'zl'=4,'core'=2,'head'=4] {'core'}, dimensions={0}, use_global_device_ids=true | all-gather | bytes 786432 | tf_op jit(solution)/shard_map/all_gather | solution.py:218
  9.7 0.0 copy-done.5
  9.7 2.2 %all_gather.19.v_ref = bf16[256,1024]{1,0:T(8,128)(2,1)S(1)} all-gather(bf16[128,1024]{1,0:T(8,128)(2,1)S(1)} %copy-done.5), channel_id=1, replica_groups=mesh['x'=4,'zh'=4,'zl'=4,'core'=2,'head'=4] {'core'}, dimensions={0}, use_global_device_ids=true | all-gather | bytes 786432 | tf_op jit(solution)/shard_map/all_gather | solution.py:218
  11.8 1.0 shard_map.84
  12.8 0.0 copy-start.6
  12.8 6.2 %all-to-all-start = ((bf16[16,32,128]{2,1,0:T(8,128)(2,1)}), bf16[16,32,128]{2,1,0:T(8,128)(2,1)S(1)}, u32[]{:S(2)}, u32[]{:S(2)}) async-start(bf16[16,32,128]{2,1,0:T(8,128)(2,1)} %bitcast.2), calls=%async_computation | async-start | bytes 262144 | tf_op jit(solution)/shard_map/all_to_all | solution.py:202
  19.0 0.0 copy-done.6
  19.0 2.7 %all_gather.20.q_ref = bf16[256,1024]{1,0:T(8,128)(2,1)S(1)} all-gather(bf16[128,1024]{1,0:T(8,128)(2,1)S(1)} %copy-done.6), channel_id=1, replica_groups=mesh['x'=4,'zh'=4,'zl'=4,'core'=2,'head'=4] {'core'}, dimensions={0}, use_global_device_ids=true | all-gather | bytes 786432 | tf_op jit(solution)/shard_map/all_gather | solution.py:218
  21.8 0.4 all-to-all-done
  22.2 0.0 copy-start.7
  22.2 0.7 shard_map.85
  22.8 12.4 %all-to-all-start.1 = ((bf16[4,128,128]{2,1,0:T(8,128)(2,1)}), bf16[4,128,128]{2,1,0:T(8,128)(2,1)S(1)}, u32[]{:S(2)}, u32[]{:S(2)}) async-start(bf16[4,128,128]{2,1,0:T(8,128)(2,1)} %bitcast.4), calls=%async_computation.1 | async-start | bytes 262144 | tf_op jit(solution)/shard_map/all_to_all | solution.py:210
  35.3 0.0 copy-done.7
  35.3 0.0 copy-start.4
  35.3 4.1 %all_gather.21.c_ref = bf16[256,1024]{1,0:T(8,128)(2,1)S(1)} all-gather(bf16[128,1024]{1,0:T(8,128)(2,1)S(1)} %copy-done.7), channel_id=1, replica_groups=mesh['x'=4,'zh'=4,'zl'=4,'core'=2,'head'=4] {'core'}, dimensions={0}, use_global_device_ids=true | all-gather | bytes 786432 | tf_op jit(solution)/shard_map/all_gather | solution.py:218
  39.4 0.0 copy-done.4
  39.4 0.7 shard_map.87
  40.1 0.0 all-to-all-done.1
  40.1 0.1 shard_map.86
  40.2 10.4 %all_to_all.77 = bf16[16,32,128]{2,1,0:T(8,128)(2,1)S(1)} all-to-all(bf16[16,32,128]{2,1,0:T(8,128)(2,1)S(1)} %bitcast.27), channel_id=1, replica_groups={{272,264,280,256,400,392,408,384,16,8,24,0,144,136,152,128},{273,265,28..., dimensions={0} | all-to-all | bytes 262144 | tf_op jit(solution)/shard_map/all_to_all | solution.py:202
  50.6 0.4 shard_map.88
  51.0 10.8 %all_to_all.78 = f32[8,8,128]{2,1,0:T(8,128)S(1)} all-to-all(f32[8,8,128]{2,1,0:T(8,128)S(1)} %bitcast.29), channel_id=1, replica_groups={{2,6,3,7,0,4,1,5},{10,14,11,15,8,12,9,13},{18,22,19,23,16,20,17,21},{26..., dimensions={0} | all-to-all | bytes 65536 | tf_op jit(solution)/shard_map/all_to_all | solution.py:241
  61.7 1.1 %shard_map.89 = (bf16[256,512]{1,0:T(8,128)(2,1)S(1)}, bf16[256,512]{1,0:T(8,128)(2,1)S(1)}, bf16[512,128]{1,0:T(8,128)(2,1)}) custom-call(s32[1]{0:T(128)} %bitcast.1.core_ref, f32[64,128]{1,0:T(8,128)S(1)} %bitcast.28, f32[256,512]{1,0:T(8,128)S(1)} %get-tuple-element.43.att_ref, bf16[256,1024]{1,0:T(8,128)(2,1)S(1)} %all_gather.20.q_ref, ...), custom_call_target="tpu_custom_call" | custom-call | flops 33554432 | bytes 2359296 | tf_op jit(solution)/shard_map/pallas_call | solution.py:242
  62.8 0.0 copy-start
  62.8 0.7 copy-done
  63.5 6.8 %all-to-all-start.4 = ((bf16[16,32,128]{2,1,0:T(8,128)(2,1)}), bf16[16,32,128]{2,1,0:T(8,128)(2,1)S(1)}, u32[]{:S(2)}, u32[]{:S(2)}) async-start(bf16[16,32,128]{2,1,0:T(8,128)(2,1)} %bitcast.11), calls=%async_computation.4 | async-start | bytes 262144 | tf_op jit(solution)/shard_map/all_to_all | solution.py:202
  70.4 0.0 copy-start.1
  70.4 0.9 copy-done.1
  71.3 2.1 %shard_map.91 = (bf16[256,512]{1,0:T(8,128)(2,1)S(1)}, bf16[256,512]{1,0:T(8,128)(2,1)S(1)}, f32[256,512]{1,0:T(8,128)S(1)}, f32[256,512]{1,0:T(8,128)S(1)}, bf16[256,512]{1,0:T(8,128)(2,1)}) custom-call(s32[1]{0:T(128)} %bitcast.1.core_ref, bf16[256,1024]{1,0:T(8,128)(2,1)S(1)} %all_gather.20.q_ref, bf16[256,1024]{1,0:T(8,128)(2,1)S(1)} %all_gather.18.k_ref, ...), custom_call_target="tpu_custom_call" | custom-call | flops 402653184 | bytes 4718592 | tf_op jit(solution)/shard_map/pallas_call | solution.py:245
  73.4 0.0 copy-start.2
  73.4 0.7 copy-done.2
  74.1 0.0 all-to-all-done.4
  74.1 0.7 shard_map.90
  74.8 11.4 %all-to-all-start.5 = ((bf16[4,128,128]{2,1,0:T(8,128)(2,1)}), bf16[4,128,128]{2,1,0:T(8,128)(2,1)S(1)}, u32[]{:S(2)}, u32[]{:S(2)}) async-start(bf16[4,128,128]{2,1,0:T(8,128)(2,1)} %bitcast.13), calls=%async_computation.5 | async-start | bytes 262144 | tf_op jit(solution)/shard_map/all_to_all | solution.py:210
  86.3 0.0 copy-start.3
  86.3 3.9 %all_gather.22.sent_ref = bf16[512,512]{1,0:T(8,128)(2,1)S(1)} all-gather(bf16[256,512]{1,0:T(8,128)(2,1)S(1)} %get-tuple-element.52), channel_id=1, replica_groups=mesh['x'=4,'zh'=4,'zl'=4,'core'=2,'head'=4] {'core'}, dimensions={0}, use_global_device_ids=true | all-gather | bytes 786432 | tf_op jit(solution)/shard_map/all_gather | solution.py:218
  90.2 0.0 copy-done.3
  90.2 0.8 shard_map.93
  91.0 0.0 all-to-all-done.5
  91.0 0.1 shard_map.92
  91.1 9.9 %all_to_all.79 = bf16[16,32,128]{2,1,0:T(8,128)(2,1)S(1)} all-to-all(bf16[16,32,128]{2,1,0:T(8,128)(2,1)S(1)} %bitcast.26), channel_id=1, replica_groups={{272,264,280,256,400,392,408,384,16,8,24,0,144,136,152,128},{273,265,28..., dimensions={0} | all-to-all | bytes 262144 | tf_op jit(solution)/shard_map/all_to_all | solution.py:202
  101.0 0.4 shard_map.94
  101.3 5.2 %all_gather.23.sent_ref = bf16[512,512]{1,0:T(8,128)(2,1)S(1)} all-gather(bf16[256,512]{1,0:T(8,128)(2,1)S(1)} %get-tuple-element.61), channel_id=1, replica_groups=mesh['x'=4,'zh'=4,'zl'=4,'core'=2,'head'=4] {'core'}, dimensions={0}, use_global_device_ids=true | all-gather | bytes 786432 | tf_op jit(solution)/shard_map/all_gather | solution.py:218
  106.6 0.8 shard_map.95
Async XLA Ops:
  0.6 9.0 %copy-start.5 = (bf16[128,1024]{1,0:T(8,128)(2,1)S(1)}, bf16[128,1024]{1,0:T(8,128)(2,1)}, u32[]{:S(2)}) copy-start(bf16[128,1024]{1,0:T(8,128)(2,1)} %param.7) | copy-start | bytes 786436
  12.8 6.2 %copy-start.6 = (bf16[128,1024]{1,0:T(8,128)(2,1)S(1)}, bf16[128,1024]{1,0:T(8,128)(2,1)}, u32[]{:S(2)}) copy-start(bf16[128,1024]{1,0:T(8,128)(2,1)} %param.5) | copy-start | bytes 786436
  12.8 9.3 %all-to-all-start = ((bf16[16,32,128]{2,1,0:T(8,128)(2,1)}), bf16[16,32,128]{2,1,0:T(8,128)(2,1)S(1)}, u32[]{:S(2)}, u32[]{:S(2)}) async-start(bf16[16,32,128]{2,1,0:T(8,128)(2,1)} %bitcast.2), calls=%async_computation | async-start | bytes 262144 | tf_op jit(solution)/shard_map/all_to_all | solution.py:202
  22.2 13.1 %copy-start.7 = (bf16[128,1024]{1,0:T(8,128)(2,1)S(1)}, bf16[128,1024]{1,0:T(8,128)(2,1)}, u32[]{:S(2)}) copy-start(bf16[128,1024]{1,0:T(8,128)(2,1)} %param.9) | copy-start | bytes 786436
  22.8 17.3 %all-to-all-start.1 = ((bf16[4,128,128]{2,1,0:T(8,128)(2,1)}), bf16[4,128,128]{2,1,0:T(8,128)(2,1)S(1)}, u32[]{:S(2)}, u32[]{:S(2)}) async-start(bf16[4,128,128]{2,1,0:T(8,128)(2,1)} %bitcast.4), calls=%async_computation.1 | async-start | bytes 262144 | tf_op jit(solution)/shard_map/all_to_all | solution.py:210
  35.3 4.1 %copy-start.4 = (f32[1024]{0:T(1024)S(1)}, f32[1024]{0:T(1024)}, u32[]{:S(2)}) copy-start(f32[1024]{0:T(1024)} %param.8) | copy-start | bytes 12292
  62.8 0.7 copy-start
  63.5 10.6 %all-to-all-start.4 = ((bf16[16,32,128]{2,1,0:T(8,128)(2,1)}), bf16[16,32,128]{2,1,0:T(8,128)(2,1)S(1)}, u32[]{:S(2)}, u32[]{:S(2)}) async-start(bf16[16,32,128]{2,1,0:T(8,128)(2,1)} %bitcast.11), calls=%async_computation.4 | async-start | bytes 262144 | tf_op jit(solution)/shard_map/all_to_all | solution.py:202
  70.4 0.9 copy-start.1
  73.4 0.7 copy-start.2
  74.8 16.2 %all-to-all-start.5 = ((bf16[4,128,128]{2,1,0:T(8,128)(2,1)}), bf16[4,128,128]{2,1,0:T(8,128)(2,1)S(1)}, u32[]{:S(2)}, u32[]{:S(2)}) async-start(bf16[4,128,128]{2,1,0:T(8,128)(2,1)} %bitcast.13), calls=%async_computation.5 | async-start | bytes 262144 | tf_op jit(solution)/shard_map/all_to_all | solution.py:210
  86.3 3.9 %copy-start.3 = (bf16[256,512]{1,0:T(8,128)(2,1)S(1)}, bf16[256,512]{1,0:T(8,128)(2,1)}, u32[]{:S(2)}) copy-start(bf16[256,512]{1,0:T(8,128)(2,1)} %copy-done.2) | copy-start | bytes 786436

commit v5 on v4

v5 whole, which is shorter than its diff:
```python
import functools

import jax
import jax.numpy as jnp
from jax import lax
from jax.experimental import pallas as pl
from jax.experimental.pallas import tpu as pltpu
from jax.sharding import Mesh, PartitionSpec as P

HEADS = 32
DH = 128
ROWS = 128
X, ZH, ZL, CORES, GROUPS = 4, 4, 4, 2, 4
LOCAL = HEADS // GROUPS
HALF = LOCAL // CORES
CHUNK = CORES * ROWS
WIDTH = LOCAL * DH
PART = HALF * DH
WIDTH_ALL = HEADS * DH
EPSILON = 1e-06
PIECE = PART // (X * ZL)
X_ORDER = (2, 1, 3, 0)
ZL_ORDER = (2, 1, 3, 0)
ZH_ORDER = (2, 1, 3, 0)
SUM_ORDER = [2, 6, 3, 7, 0, 4, 1, 5]
PLANE = [[x * ZL + z for x in X_ORDER for z in ZL_ORDER]]
F32 = jnp.float32
BF16 = jnp.bfloat16

VMEM = pl.BlockSpec(memory_space=pltpu.VMEM)
SMEM = pl.BlockSpec(memory_space=pltpu.SMEM)
ANY = pl.BlockSpec(memory_space=pl.ANY)


def dot(a, b, ca, cb):
    return lax.dot_general(a, b, (((ca,), (cb,)), ((), ())), preferred_element_type=F32)


def at(h):
    return slice(h * DH, (h + 1) * DH)


def part_of(core, size):
    return pl.ds(pl.multiple_of(core * size, size), size)


def causal():
    t = lax.broadcasted_iota(jnp.int32, (CHUNK, CHUNK), 0)
    s = lax.broadcasted_iota(jnp.int32, (CHUNK, CHUNK), 1)
    return s <= t


def call(kernel, shapes, flops, moved, specs, scratch=(), out=VMEM):
    return pl.pallas_call(
        kernel,
        out_shape=[jax.ShapeDtypeStruct(s, d) for s, d in shapes],
        in_specs=specs,
        out_specs=[out] * len(shapes),
        scratch_shapes=scratch,
        compiler_params=pltpu.CompilerParams(vmem_limit_bytes=32 * 1024 * 1024),
        cost_estimate=pl.CostEstimate(flops=flops, bytes_accessed=moved, transcendentals=0),
    )


MATMUL = LOCAL * 2 * DH * DH * DH
BLOCK = ROWS * WIDTH * 2


def pack_kernel(core_ref, a_ref, b_ref, send_ref, sems):
    leaving = part_of(1 - core_ref[0], PART)
    copies = [
        pltpu.make_async_copy(ref.at[:, leaving], send_ref.at[pl.ds(i * ROWS, ROWS), :], sems.at[i])
        for i, ref in enumerate((a_ref, b_ref))
    ]
    for copy in copies:
        copy.start()
    for copy in copies:
        copy.wait()


def arrived(core, sent_ref, i):
    other = 1 - core
    return sent_ref[pl.ds(pl.multiple_of(other * CHUNK + i * ROWS, ROWS), ROWS), :]


def assemble(core, own_ref, sent_ref, i, near_ref):
    near_ref[part_of(core, ROWS), :] = own_ref[:, part_of(core, PART)]
    near_ref[part_of(1 - core, ROWS), :] = arrived(core, sent_ref, i)


def states_kernel(core_ref, k_ref, v_ref, sent_ref, k_near_ref, v_near_ref, mine_ref):
    assemble(core_ref[0], k_ref, sent_ref, 0, k_near_ref)
    assemble(core_ref[0], v_ref, sent_ref, 1, v_near_ref)
    for h in range(HALF):
        mine_ref[at(h), :] = dot(k_near_ref[:, at(h)], v_near_ref[:, at(h)], 0, 0).astype(BF16)


def spot(x, z):
    return (X_ORDER.index(x) * ZL + ZL_ORDER.index(z)) * PIECE


def piece(ref, start):
    return ref[start : start + PIECE, :].astype(F32)


def cube_kernel(in_ref, out_ref):
    for x in range(X):
        total = piece(in_ref, spot(x, 0))
        for z in range(1, ZL):
            total = total + piece(in_ref, spot(x, z))
        total = total.astype(BF16)
        for copy in range(ZH):
            start = (copy * X + x) * PIECE
            out_ref[start : start + PIECE, :] = total


def scan_kernel(reverse, place_ref, in_ref, cubes_ref, out_ref):
    here = place_ref[0]
    order = (lambda n: reversed(range(n))) if reverse else range
    column = jnp.zeros((PIECE, DH), F32)
    for x in order(X):
        total = column
        for z in range(ZH):
            cube = piece(cubes_ref, (ZH_ORDER.index(z) * X + x) * PIECE)
            column = column + cube
            ahead = here < z if reverse else here > z
            total = total + jnp.where(ahead, cube, 0.0)
        for z in order(ZL):
            start = spot(x, z)
            out_ref[start : start + PIECE, :] = total.astype(BF16)
            total = total + piece(in_ref, start)


def inside_kernel(
    core_ref, q_ref, c_ref, sent_ref, k_ref, v_ref, gain_ref, q_near_ref, inside_ref, weighted_ref, near_gain_ref
):
    core = core_ref[0]
    mask = causal()
    assemble(core, q_ref, sent_ref, 0, q_near_ref)
    gain = gain_ref[:, part_of(core, PART)]
    near_gain_ref[...] = jnp.broadcast_to(gain, (8, PART))
    weighted_ref[part_of(core, ROWS), :] = c_ref[:, part_of(core, PART)].astype(F32) * gain
    weighted_ref[part_of(1 - core, ROWS), :] = arrived(core, sent_ref, 1).astype(F32) * gain
    for h in range(HALF):
        raw = dot(q_near_ref[:, at(h)], k_ref[:, at(h)], 1, 1)
        scores = jnp.where(mask, raw, 0.0).astype(BF16)
        inside_ref[:, at(h)] = dot(scores, v_ref[:, at(h)], 1, 0)


def rows_of(block):
    return [jnp.sum(block[i * ROWS : (i + 1) * ROWS].T, axis=0, keepdims=True) for i in range(CORES)]


def attended_kernel(q_ref, inside_ref, before_ref, weighted_ref, att_ref, sums_ref):
    squares = jnp.zeros((CHUNK, DH), F32)
    crossed = jnp.zeros((CHUNK, DH), F32)
    for h in range(HALF):
        att = inside_ref[:, at(h)] + dot(q_ref[:, at(h)], before_ref[at(h), :], 1, 0)
        att_ref[:, at(h)] = att
        squares = squares + att * att
        crossed = crossed + weighted_ref[:, at(h)] * att
    block = jnp.concatenate(rows_of(squares) + rows_of(crossed) + [jnp.zeros((4, ROWS), F32)], axis=0)
    for i in range(CORES * GROUPS):
        sums_ref[i * 8 : (i + 1) * 8, :] = block


def tall(rows):
    return jnp.concatenate([jnp.broadcast_to(row, (ROWS, ROWS)).T for row in rows], axis=0)


def token_scales(sums_ref):
    sums = sums_ref[0:8, :]
    for i in range(1, CORES * GROUPS):
        sums = sums + sums_ref[i * 8 : (i + 1) * 8, :]
    inverse_rows = lax.rsqrt(sums[0:2] / WIDTH_ALL + EPSILON)
    cubed_rows = inverse_rows * inverse_rows * inverse_rows * (sums[2:4] / WIDTH_ALL)
    return tall([inverse_rows[0:1], inverse_rows[1:2]]), tall([cubed_rows[0:1], cubed_rows[1:2]])


def grad_of(inverse, cubed, weighted_ref, att_ref, h):
    return (inverse * weighted_ref[:, at(h)] - cubed * att_ref[:, at(h)]).astype(BF16)


def products_kernel(sums_ref, att_ref, q_ref, weighted_ref, mine_ref):
    inverse, cubed = token_scales(sums_ref)
    for h in range(HALF):
        g = grad_of(inverse, cubed, weighted_ref, att_ref, h)
        mine_ref[at(h), :] = dot(q_ref[:, at(h)], g, 0, 0).astype(BF16)


def local_grads_kernel(
    core_ref, sums_ref, att_ref, weighted_ref, gain_ref, q_ref, k_ref, v_ref, before_ref,
    keep_ref, send_ref, gk_ref, gv_ref, normed_ref, gq_ref,
):
    mask = causal()
    inverse, cubed = token_scales(sums_ref)
    for h in range(HALF):
        q, k, v = q_ref[:, at(h)], k_ref[:, at(h)], v_ref[:, at(h)]
        normed_ref[:, at(h)] = (att_ref[:, at(h)] * inverse * gain_ref[0:1, at(h)]).astype(BF16)
        g = grad_of(inverse, cubed, weighted_ref, att_ref, h)
        scores = jnp.where(mask, dot(q, k, 1, 1), 0.0).astype(BF16)
        grad_scores = jnp.where(mask, dot(g, v, 1, 1), 0.0).astype(BF16)
        gq_ref[:, at(h)] = (dot(grad_scores, k, 1, 0) + dot(g, before_ref[at(h), :], 1, 1)).astype(BF16)
        gk_ref[:, at(h)] = dot(grad_scores, q, 0, 0)
        gv_ref[:, at(h)] = dot(scores, g, 0, 0)
    for out_ref, core in ((keep_ref, core_ref[0]), (send_ref, 1 - core_ref[0])):
        out_ref[0:ROWS, :] = normed_ref[part_of(core, ROWS), :]
        out_ref[ROWS : 2 * ROWS, :] = gq_ref[part_of(core, ROWS), :]


def last_kernel(core_ref, k_ref, v_ref, gk_part_ref, gv_part_ref, beyond_ref, keep_ref, send_ref):
    for h in range(HALF):
        beyond = beyond_ref[at(h), :]
        for out_ref, core in ((keep_ref, core_ref[0]), (send_ref, 1 - core_ref[0])):
            rows = part_of(core, ROWS)
            gk = gk_part_ref[rows, at(h)] + dot(v_ref[rows, at(h)], beyond, 1, 1)
            gv = gv_part_ref[rows, at(h)] + dot(k_ref[rows, at(h)], beyond, 1, 0)
            out_ref[0:ROWS, at(h)] = gk.astype(BF16)
            out_ref[ROWS : 2 * ROWS, at(h)] = gv.astype(BF16)


def join_kernel(core_ref, keep_ref, sent_ref, first_ref, second_ref):
    core = core_ref[0]
    for i, out_ref in enumerate((first_ref, second_ref)):
        out_ref[:, part_of(core, PART)] = keep_ref[i * ROWS : (i + 1) * ROWS, :]
        out_ref[:, part_of(1 - core, PART)] = arrived(core, sent_ref, i)


FLAT = (PART, DH)
TALL = (CHUNK, PART)
OUT = (ROWS, WIDTH)


def plane_swap(a):
    return lax.all_to_all(a, ("x", "zl"), 0, 0, axis_index_groups=PLANE, tiled=True)


def chips_scan(mine, reverse, beside_turn=lambda: None, beside_cubes=lambda: None):
    place = lax.axis_index("zh").reshape(1).astype(jnp.int32)
    turned = plane_swap(mine)
    (cube,) = call(cube_kernel, [(FLAT, BF16)], 0, BLOCK, [VMEM])(turned)
    cube, extra = lax.optimization_barrier((cube, beside_turn()))
    cubes = lax.all_to_all(cube, "zh", 0, 0, axis_index_groups=[list(ZH_ORDER)], tiled=True)
    scan = functools.partial(scan_kernel, reverse)
    (summed,) = call(scan, [(FLAT, BF16)], 0, 2 * BLOCK, [SMEM, VMEM, VMEM])(place, turned, cubes)
    summed, more = lax.optimization_barrier((summed, beside_cubes()))
    return plane_swap(summed), extra, more


def pair(a):
    return lax.all_gather(a, "core", axis=0, tiled=True)


def joined(core, keep, send):
    return call(join_kernel, [(OUT, BF16), (OUT, BF16)], 0, 4 * BLOCK, [SMEM, VMEM, VMEM])(core, keep, pair(send))


def swapped(core, a, b):
    (send,) = call(
        pack_kernel, [(TALL, BF16)], 0, 2 * BLOCK, [SMEM, ANY, ANY], [pltpu.SemaphoreType.DMA((2,))], ANY
    )(core, a, b)
    return pair(send)


def local(q, k, v, gain, c):
    core = lax.axis_index("core").reshape(1).astype(jnp.int32)
    gain = gain.reshape(1, WIDTH)
    k, v, mine = call(
        states_kernel, [(TALL, BF16), (TALL, BF16), (FLAT, BF16)], MATMUL, 5 * BLOCK, [SMEM] + [VMEM] * 3
    )(core, k, v, swapped(core, k, v))
    sent = swapped(core, q, c)

    def prepare():
        return call(
            inside_kernel,
            [(TALL, BF16), (TALL, F32), (TALL, F32), ((8, PART), F32)],
            4 * MATMUL, 12 * BLOCK, [SMEM] + [VMEM] * 6,
        )(core, q, c, sent, k, v, gain)

    before, sent, (q_near, inside, weighted, near_gain) = chips_scan(mine, False, lambda: sent, prepare)
    att, sums = call(
        attended_kernel, [(TALL, F32), ((CORES * GROUPS * 8, ROWS), F32)], MATMUL, 10 * BLOCK, [VMEM] * 4
    )(q_near, inside, before, weighted)
    sums = lax.all_to_all(sums, ("core", "head"), 0, 0, axis_index_groups=[SUM_ORDER], tiled=True)
    (mine,) = call(products_kernel, [(FLAT, BF16)], MATMUL, 6 * BLOCK, [VMEM] * 4)(sums, att, q_near, weighted)
    keep, send, gk_part, gv_part = call(
        local_grads_kernel,
        [(TALL, BF16), (TALL, BF16), (TALL, F32), (TALL, F32)],
        12 * MATMUL, 18 * BLOCK, [SMEM] + [VMEM] * 8, [pltpu.VMEM(TALL, BF16)] * 2,
    )(core, sums, att, weighted, near_gain, q_near, k, v, before)
    beyond, (gk_part, gv_part), (normed, gq) = chips_scan(
        mine, True, lambda: (gk_part, gv_part), lambda: joined(core, keep, send)
    )
    keep, send = call(last_kernel, [(TALL, BF16), (TALL, BF16)], 2 * MATMUL, 11 * BLOCK, [SMEM] + [VMEM] * 5)(
        core, k, v, gk_part, gv_part, beyond
    )
    gk, gv = joined(core, keep, send)
    return normed, gq, gk, gv


def solution(mesh):
    fine = Mesh(mesh.devices.reshape(X, ZH, ZL, CORES, GROUPS), ("x", "zh", "zl", "core", "head"))
    block = P(("x", "zh", "zl", "core"), "head")
    return jax.shard_map(
        local, mesh=fine, in_specs=(block, block, block, P("head"), block), out_specs=(block,) * 4, check_vma=False
    )
```

time: 108 us -> 107 us (level)
  blocking collectives: 58.4 us -> 54.5 us
  waiting for transfers between devices: 0.4 us -> 2.67 us
    all_gather x6 -> x4, blocking collectives: 27.2 us -> 21 us  [pair(): return lax.all_gather(a, 'core', axis=0, tiled=True)]
    all_to_all x2, blocking collectives: 20.3 us -> 22.8 us  [plane_swap(): lax.all_to_all(a, ('x', 'zl'), 0, 0, axis_index_groups=PLANE, tiled=True)]
    all_to_all x2, waiting for transfers between devices: 0.39 us -> 1.56 us  [plane_swap(): lax.all_to_all(a, ('x', 'zl'), 0, 0, axis_index_groups=PLANE, tiled=True)]
    all_to_all x2, waiting for transfers between devices: 0.01 us -> 1.11 us  [chips_scan(): lax.all_to_all(cube, 'zh', 0, 0, axis_index_groups=[list(ZH_ORDER)], tile...]
    unnamed x16 -> x14, local copies, waits for them, and re-layouts: 2.37 us -> 3.29 us
    pallas_call x3 -> x5, Pallas kernels: 2.76 us -> 2.77 us  [the longest x1 1.03 us: local(): call(products_kernel, [(FLAT, BF16)], MATMUL, 6 * BLOCK, [VMEM] * 4)]
  transfers between devices with their start and end apart: 4 -> 4, of which waited for: 1 -> 3; matrix products, arithmetic and copies ran while one was open for 0% -> 0% of each run, Pallas kernels for 3% -> 3%
where the time goes in v5:
time: 107 us; the launch traced here: 106 us
  blocking collectives  54.5 us (51%)
  starting transfers between devices  36.8 us (34%)
  Pallas kernels  8.13 us (8%)
  local copies, waits for them, and re-layouts  3.29 us (3%)
  waiting for transfers between devices  2.67 us (2%)
    all_to_all x2, starting transfers between devices, chips_scan(): lax.all_to_all(cube, 'zh', 0, 0, axis_index_groups=[list(ZH_ORDER)], tile...  23.9 us
    all_to_all x2, blocking collectives, plane_swap(): lax.all_to_all(a, ('x', 'zl'), 0, 0, axis_index_groups=PLANE, tiled=True)  22.8 us
    all_gather x4, blocking collectives, pair(): return lax.all_gather(a, 'core', axis=0, tiled=True)  21 us
    all_to_all x2, starting transfers between devices, plane_swap(): lax.all_to_all(a, ('x', 'zl'), 0, 0, axis_index_groups=PLANE, tiled=True)  12.9 us
    all_to_all x1, blocking collectives, local(): lax.all_to_all(sums, ('core', 'head'), 0, 0, axis_index_groups=[SUM_ORDER...  10.8 us
    unnamed x14, local copies, waits for them, and re-layouts  3.29 us
  transfers between devices with their start and end apart: 4, of which 3 were waited for; matrix products, arithmetic and copies ran while one was open for 0% of the time, Pallas kernels for 3%

profile of v5, /device:TPU:1, one launch (start us, length us, event | category | flops | bytes accessed | tf_op | source)
XLA Modules:
  0.0 106.1 jit_solution(11294978679907729424)
XLA Ops:
  0.6 0.0 copy-start
  0.6 0.9 copy-done
  1.6 0.0 copy-start.1
  1.6 0.9 copy-done.1
  2.5 0.1 shard_map.84
  2.6 8.7 %all_gather.12.sent_ref = bf16[512,512]{1,0:T(8,128)(2,1)S(1)} all-gather(bf16[256,512]{1,0:T(8,128)(2,1)S(1)} %shard_map.84), channel_id=1, replica_groups=mesh['x'=4,'zh'=4,'zl'=4,'core'=2,'head'=4] {'core'}, dimensions={0}, use_global_device_ids=true | all-gather | bytes 786432 | tf_op jit(solution)/shard_map/all_gather | solution.py:251
  11.3 0.0 copy-start.3
  11.3 1.0 shard_map.85
  12.3 0.0 copy-start.2
  12.3 6.2 %all-to-all-start = ((bf16[16,32,128]{2,1,0:T(8,128)(2,1)}), bf16[16,32,128]{2,1,0:T(8,128)(2,1)S(1)}, u32[]{:S(2)}, u32[]{:S(2)}) async-start(bf16[16,32,128]{2,1,0:T(8,128)(2,1)} %bitcast.2), calls=%async_computation | async-start | bytes 262144 | tf_op jit(solution)/shard_map/all_to_all | solution.py:235
  18.4 0.0 copy-done.3
  18.5 0.0 copy-done.2
  18.5 0.1 shard_map.87
  18.5 2.7 %all_gather.13.sent_ref = bf16[512,512]{1,0:T(8,128)(2,1)S(1)} all-gather(bf16[256,512]{1,0:T(8,128)(2,1)S(1)} %shard_map.87), channel_id=1, replica_groups=mesh['x'=4,'zh'=4,'zl'=4,'core'=2,'head'=4] {'core'}, dimensions={0}, use_global_device_ids=true | all-gather | bytes 786432 | tf_op jit(solution)/shard_map/all_gather | solution.py:251
  21.3 0.5 all-to-all-done
  21.8 0.7 shard_map.86
  22.4 12.4 %all-to-all-start.1 = ((bf16[4,128,128]{2,1,0:T(8,128)(2,1)}), bf16[4,128,128]{2,1,0:T(8,128)(2,1)S(1)}, u32[]{:S(2)}, u32[]{:S(2)}) async-start(bf16[4,128,128]{2,1,0:T(8,128)(2,1)} %bitcast.4), calls=%async_computation.1 | async-start | bytes 262144 | tf_op jit(solution)/shard_map/all_to_all | solution.py:243
  34.9 0.0 copy-start.6
  34.9 0.7 copy-done.6
  35.6 0.7 shard_map.89
  36.2 1.1 %all-to-all-done.1 = bf16[4,128,128]{2,1,0:T(8,128)(2,1)S(1)} async-done(((bf16[4,128,128]{2,1,0:T(8,128)(2,1)}), bf16[4,128,128]{2,1,0:T(8,128)(2,1)S(1)}, u32[]{:S(2)}, u32[]{:S(2)}) %all-to-all-start.1) | async-done | bytes 131104 | tf_op jit(solution)/shard_map/all_to_all | solution.py:243
  37.3 0.1 shard_map.88
  37.4 12.9 %all_to_all.77 = bf16[16,32,128]{2,1,0:T(8,128)(2,1)S(1)} all-to-all(bf16[16,32,128]{2,1,0:T(8,128)(2,1)S(1)} %bitcast.27), channel_id=1, replica_groups={{272,264,280,256,144,136,152,128,400,392,408,384,16,8,24,0},{273,265,28..., dimensions={0} | all-to-all | bytes 262144 | tf_op jit(solution)/shard_map/all_to_all | solution.py:235
  50.2 0.3 shard_map.90
  50.6 10.8 %all_to_all.78 = f32[8,8,128]{2,1,0:T(8,128)S(1)} all-to-all(f32[8,8,128]{2,1,0:T(8,128)S(1)} %bitcast.30), channel_id=1, replica_groups={{2,6,3,7,0,4,1,5},{10,14,11,15,8,12,9,13},{18,22,19,23,16,20,17,21},{26..., dimensions={0} | all-to-all | bytes 65536 | tf_op jit(solution)/shard_map/all_to_all | solution.py:284
  61.4 1.0 shard_map.91
  62.4 6.7 %all-to-all-start.4 = ((bf16[16,32,128]{2,1,0:T(8,128)(2,1)}), bf16[16,32,128]{2,1,0:T(8,128)(2,1)S(1)}, u32[]{:S(2)}, u32[]{:S(2)}) async-start(bf16[16,32,128]{2,1,0:T(8,128)(2,1)} %bitcast.11), calls=%async_computation.4 | async-start | bytes 262144 | tf_op jit(solution)/shard_map/all_to_all | solution.py:235
  69.1 1.5 %shard_map.93 = (bf16[256,512]{1,0:T(8,128)(2,1)S(1)}, bf16[256,512]{1,0:T(8,128)(2,1)S(1)}, f32[256,512]{1,0:T(8,128)S(1)}, f32[256,512]{1,0:T(8,128)S(1)}) custom-call(s32[1]{0:T(128)} %bitcast.1.core_ref, f32[64,128]{1,0:T(8,128)S(1)} %bitcast.29, f32[256,512]{1,0:T(8,128)S(1)} %get-tuple-element.48.att_ref, ...), custom_call_target="tpu_custom_call" | custom-call | flops 402653184 | bytes 4718592 | tf_op jit(solution)/shard_map/pallas_call | solution.py:286
  70.6 0.0 copy-start.4
  70.6 0.7 copy-done.4
  71.3 1.1 %all-to-all-done.4 = bf16[16,32,128]{2,1,0:T(8,128)(2,1)S(1)} async-done(((bf16[16,32,128]{2,1,0:T(8,128)(2,1)}), bf16[16,32,128]{2,1,0:T(8,128)(2,1)S(1)}, u32[]{:S(2)}, u32[]{:S(2)}) %all-to-all-start.4) | async-done | bytes 131104 | tf_op jit(solution)/shard_map/all_to_all | solution.py:235
  72.4 0.7 shard_map.92
  73.1 11.4 %all-to-all-start.5 = ((bf16[4,128,128]{2,1,0:T(8,128)(2,1)}), bf16[4,128,128]{2,1,0:T(8,128)(2,1)S(1)}, u32[]{:S(2)}, u32[]{:S(2)}) async-start(bf16[4,128,128]{2,1,0:T(8,128)(2,1)} %bitcast.13), calls=%async_computation.5 | async-start | bytes 262144 | tf_op jit(solution)/shard_map/all_to_all | solution.py:243
  84.5 0.0 copy-start.5
  84.5 4.5 %all_gather.14.sent_ref = bf16[512,512]{1,0:T(8,128)(2,1)S(1)} all-gather(bf16[256,512]{1,0:T(8,128)(2,1)S(1)} %get-tuple-element.54), channel_id=1, replica_groups=mesh['x'=4,'zh'=4,'zl'=4,'core'=2,'head'=4] {'core'}, dimensions={0}, use_global_device_ids=true | all-gather | bytes 786432 | tf_op jit(solution)/shard_map/all_gather | solution.py:251
  89.1 0.0 copy-done.5
  89.1 0.8 shard_map.95
  89.9 0.0 all-to-all-done.5
  89.9 0.1 shard_map.94
  89.9 9.9 %all_to_all.79 = bf16[16,32,128]{2,1,0:T(8,128)(2,1)S(1)} all-to-all(bf16[16,32,128]{2,1,0:T(8,128)(2,1)S(1)} %bitcast.26), channel_id=1, replica_groups={{272,264,280,256,144,136,152,128,400,392,408,384,16,8,24,0},{273,265,28..., dimensions={0} | all-to-all | bytes 262144 | tf_op jit(solution)/shard_map/all_to_all | solution.py:235
  99.8 0.4 shard_map.96
  100.2 5.0 %all_gather.15.sent_ref = bf16[512,512]{1,0:T(8,128)(2,1)S(1)} all-gather(bf16[256,512]{1,0:T(8,128)(2,1)S(1)} %get-tuple-element.63), channel_id=1, replica_groups=mesh['x'=4,'zh'=4,'zl'=4,'core'=2,'head'=4] {'core'}, dimensions={0}, use_global_device_ids=true | all-gather | bytes 786432 | tf_op jit(solution)/shard_map/all_gather | solution.py:251
  105.2 0.8 shard_map.97
Async XLA Ops:
  0.6 1.0 copy-start
  1.6 0.9 copy-start.1
  11.3 7.2 %copy-start.3 = (bf16[128,1024]{1,0:T(8,128)(2,1)S(1)}, bf16[128,1024]{1,0:T(8,128)(2,1)}, u32[]{:S(2)}) copy-start(bf16[128,1024]{1,0:T(8,128)(2,1)} %c_ref.1) | copy-start | bytes 786436
  12.3 6.2 %copy-start.2 = (bf16[128,1024]{1,0:T(8,128)(2,1)S(1)}, bf16[128,1024]{1,0:T(8,128)(2,1)}, u32[]{:S(2)}) copy-start(bf16[128,1024]{1,0:T(8,128)(2,1)} %q_ref.1) | copy-start | bytes 786436
  12.3 9.5 %all-to-all-start = ((bf16[16,32,128]{2,1,0:T(8,128)(2,1)}), bf16[16,32,128]{2,1,0:T(8,128)(2,1)S(1)}, u32[]{:S(2)}, u32[]{:S(2)}) async-start(bf16[16,32,128]{2,1,0:T(8,128)(2,1)} %bitcast.2), calls=%async_computation | async-start | bytes 262144 | tf_op jit(solution)/shard_map/all_to_all | solution.py:235
  22.4 14.9 %all-to-all-start.1 = ((bf16[4,128,128]{2,1,0:T(8,128)(2,1)}), bf16[4,128,128]{2,1,0:T(8,128)(2,1)S(1)}, u32[]{:S(2)}, u32[]{:S(2)}) async-start(bf16[4,128,128]{2,1,0:T(8,128)(2,1)} %bitcast.4), calls=%async_computation.1 | async-start | bytes 262144 | tf_op jit(solution)/shard_map/all_to_all | solution.py:243
  34.9 0.7 copy-start.6
  62.4 10.0 %all-to-all-start.4 = ((bf16[16,32,128]{2,1,0:T(8,128)(2,1)}), bf16[16,32,128]{2,1,0:T(8,128)(2,1)S(1)}, u32[]{:S(2)}, u32[]{:S(2)}) async-start(bf16[16,32,128]{2,1,0:T(8,128)(2,1)} %bitcast.11), calls=%async_computation.4 | async-start | bytes 262144 | tf_op jit(solution)/shard_map/all_to_all | solution.py:235
  70.6 0.7 copy-start.4
  73.1 16.8 %all-to-all-start.5 = ((bf16[4,128,128]{2,1,0:T(8,128)(2,1)}), bf16[4,128,128]{2,1,0:T(8,128)(2,1)S(1)}, u32[]{:S(2)}, u32[]{:S(2)}) async-start(bf16[4,128,128]{2,1,0:T(8,128)(2,1)} %bitcast.13), calls=%async_computation.5 | async-start | bytes 262144 | tf_op jit(solution)/shard_map/all_to_all | solution.py:243
  84.5 4.5 %copy-start.5 = (bf16[256,512]{1,0:T(8,128)(2,1)S(1)}, bf16[256,512]{1,0:T(8,128)(2,1)}, u32[]{:S(2)}) copy-start(bf16[256,512]{1,0:T(8,128)(2,1)} %copy-done.4) | copy-start | bytes 786436

commit v6 on v5

--- a/solution.py
+++ b/solution.py
@@ -277,7 +277,7 @@
             4 * MATMUL, 12 * BLOCK, [SMEM] + [VMEM] * 6,
         )(core, q, c, sent, k, v, gain)
 
-    before, sent, (q_near, inside, weighted, near_gain) = chips_scan(mine, False, lambda: sent, prepare)
+    before, _, (q_near, inside, weighted, near_gain) = chips_scan(mine, False, lambda: None, prepare)
     att, sums = call(
         attended_kernel, [(TALL, F32), ((CORES * GROUPS * 8, ROWS), F32)], MATMUL, 10 * BLOCK, [VMEM] * 4
     )(q_near, inside, before, weighted)
@@ -288,8 +288,8 @@
         [(TALL, BF16), (TALL, BF16), (TALL, F32), (TALL, F32)],
         12 * MATMUL, 18 * BLOCK, [SMEM] + [VMEM] * 8, [pltpu.VMEM(TALL, BF16)] * 2,
     )(core, sums, att, weighted, near_gain, q_near, k, v, before)
-    beyond, (gk_part, gv_part), (normed, gq) = chips_scan(
-        mine, True, lambda: (gk_part, gv_part), lambda: joined(core, keep, send)
+    beyond, _, (gk_part, gv_part, normed, gq) = chips_scan(
+        mine, True, lambda: None, lambda: (gk_part, gv_part) + tuple(joined(core, keep, send))
     )
     keep, send = call(last_kernel, [(TALL, BF16), (TALL, BF16)], 2 * MATMUL, 11 * BLOCK, [SMEM] + [VMEM] * 5)(
         core, k, v, gk_part, gv_part, beyond

time: 107 us -> 104 us (0.972)
  blocking collectives: 54.5 us -> 70 us
  starting transfers between devices: 36.8 us -> 23.7 us
  waiting for transfers between devices: 2.67 us -> 0.01 us
  Pallas kernels: 8.13 us -> 6.8 us
    all_to_all x2 -> x4, blocking collectives: 22.8 us -> 38.8 us  [plane_swap(): lax.all_to_all(a, ('x', 'zl'), 0, 0, axis_index_groups=PLANE, tiled=True)]
    all_to_all x2 -> x0, starting transfers between devices: 12.9 us -> none  [plane_swap(): lax.all_to_all(a, ('x', 'zl'), 0, 0, axis_index_groups=PLANE, tiled=True)]
    all_to_all x2 -> x0, waiting for transfers between devices: 1.56 us -> none  [plane_swap(): lax.all_to_all(a, ('x', 'zl'), 0, 0, axis_index_groups=PLANE, tiled=True)]
    all_to_all x2, waiting for transfers between devices: 1.11 us -> 0.01 us  [chips_scan(): lax.all_to_all(cube, 'zh', 0, 0, axis_index_groups=[list(ZH_ORDER)], tile...]
    unnamed x14 -> x10, local copies, waits for them, and re-layouts: 3.29 us -> 2.59 us
  transfers between devices with their start and end apart: 4 -> 2, of which waited for: 3 -> 0; matrix products, arithmetic and copies ran while one was open for 0% -> 0% of each run, Pallas kernels for 3% -> 3%
where the time goes in v6:
time: 104 us
  blocking collectives  70 us (67%)
  starting transfers between devices  23.7 us (23%)
  Pallas kernels  6.8 us (7%)
  local copies, waits for them, and re-layouts  2.59 us (2%)
    all_to_all x4, blocking collectives, plane_swap(): lax.all_to_all(a, ('x', 'zl'), 0, 0, axis_index_groups=PLANE, tiled=True)  38.8 us
    all_to_all x2, starting transfers between devices, chips_scan(): lax.all_to_all(cube, 'zh', 0, 0, axis_index_groups=[list(ZH_ORDER)], tile...  23.7 us
    all_gather x4, blocking collectives, pair(): return lax.all_gather(a, 'core', axis=0, tiled=True)  20.9 us
    all_to_all x1, blocking collectives, local(): lax.all_to_all(sums, ('core', 'head'), 0, 0, axis_index_groups=[SUM_ORDER...  10.4 us
    unnamed x10, local copies, waits for them, and re-layouts  2.59 us
  transfers between devices with their start and end apart: 2, of which 0 were waited for; matrix products, arithmetic and copies ran while one was open for 0% of the time, Pallas kernels for 3%

profile of v6, /device:TPU:1, one launch (start us, length us, event | category | flops | bytes accessed | tf_op | source)
XLA Modules:
  0.0 103.8 jit_solution(8201284617406761077)
XLA Ops:
  0.6 0.0 copy-start
  0.6 0.9 copy-done
  1.6 0.0 copy-start.1
  1.6 0.9 copy-done.1
  2.5 0.1 shard_map.84
  2.6 8.7 %all_gather.12.sent_ref = bf16[512,512]{1,0:T(8,128)(2,1)S(1)} all-gather(bf16[256,512]{1,0:T(8,128)(2,1)S(1)} %shard_map.84), channel_id=1, replica_groups=mesh['x'=4,'zh'=4,'zl'=4,'core'=2,'head'=4] {'core'}, dimensions={0}, use_global_device_ids=true | all-gather | bytes 786432 | tf_op jit(solution)/shard_map/all_gather | solution.py:251
  11.3 0.3 shard_map.85
  11.6 9.2 %all_to_all.77 = bf16[16,32,128]{2,1,0:T(8,128)(2,1)S(1)} all-to-all(bf16[16,32,128]{2,1,0:T(8,128)(2,1)S(1)} %bitcast.31), channel_id=1, replica_groups={{272,264,280,256,144,136,152,128,400,392,408,384,16,8,24,0},{273,265,28..., dimensions={0} | all-to-all | bytes 262144 | tf_op jit(solution)/shard_map/all_to_all | solution.py:235
  20.8 0.0 copy-start.2
  20.8 0.0 copy-start.3
  20.8 0.7 shard_map.86
  21.4 12.2 %all-to-all-start.1 = ((bf16[4,128,128]{2,1,0:T(8,128)(2,1)}), bf16[4,128,128]{2,1,0:T(8,128)(2,1)S(1)}, u32[]{:S(2)}, u32[]{:S(2)}) async-start(bf16[4,128,128]{2,1,0:T(8,128)(2,1)} %bitcast.4), calls=%async_computation.1 | async-start | bytes 262144 | tf_op jit(solution)/shard_map/all_to_all | solution.py:243
  33.7 0.0 copy-done.2
  33.7 0.0 copy-done.3
  33.7 0.1 shard_map.88
  33.7 4.1 %all_gather.13.sent_ref = bf16[512,512]{1,0:T(8,128)(2,1)S(1)} all-gather(bf16[256,512]{1,0:T(8,128)(2,1)S(1)} %shard_map.88), channel_id=1, replica_groups=mesh['x'=4,'zh'=4,'zl'=4,'core'=2,'head'=4] {'core'}, dimensions={0}, use_global_device_ids=true | all-gather | bytes 786432 | tf_op jit(solution)/shard_map/all_gather | solution.py:251
  37.8 0.0 copy-start.4
  37.8 0.7 copy-done.4
  38.5 0.7 shard_map.89
  39.1 0.0 all-to-all-done.1
  39.2 0.1 shard_map.87
  39.2 10.0 %all_to_all.78 = bf16[16,32,128]{2,1,0:T(8,128)(2,1)S(1)} all-to-all(bf16[16,32,128]{2,1,0:T(8,128)(2,1)S(1)} %bitcast.28), channel_id=1, replica_groups={{272,264,280,256,144,136,152,128,400,392,408,384,16,8,24,0},{273,265,28..., dimensions={0} | all-to-all | bytes 262144 | tf_op jit(solution)/shard_map/all_to_all | solution.py:235
  49.2 0.3 shard_map.90
  49.6 10.4 %all_to_all.79 = f32[8,8,128]{2,1,0:T(8,128)S(1)} all-to-all(f32[8,8,128]{2,1,0:T(8,128)S(1)} %bitcast.32), channel_id=1, replica_groups={{2,6,3,7,0,4,1,5},{10,14,11,15,8,12,9,13},{18,22,19,23,16,20,17,21},{26..., dimensions={0} | all-to-all | bytes 65536 | tf_op jit(solution)/shard_map/all_to_all | solution.py:284
  60.0 0.4 shard_map.91
  60.3 9.8 %all_to_all.80 = bf16[16,32,128]{2,1,0:T(8,128)(2,1)S(1)} all-to-all(bf16[16,32,128]{2,1,0:T(8,128)(2,1)S(1)} %bitcast.24), channel_id=1, replica_groups={{272,264,280,256,144,136,152,128,400,392,408,384,16,8,24,0},{273,265,28..., dimensions={0} | all-to-all | bytes 262144 | tf_op jit(solution)/shard_map/all_to_all | solution.py:235
  70.2 0.7 shard_map.92
  70.8 11.4 %all-to-all-start.5 = ((bf16[4,128,128]{2,1,0:T(8,128)(2,1)}), bf16[4,128,128]{2,1,0:T(8,128)(2,1)S(1)}, u32[]{:S(2)}, u32[]{:S(2)}) async-start(bf16[4,128,128]{2,1,0:T(8,128)(2,1)} %bitcast.13), calls=%async_computation.5 | async-start | bytes 262144 | tf_op jit(solution)/shard_map/all_to_all | solution.py:243
  82.3 1.5 %shard_map.94 = (bf16[256,512]{1,0:T(8,128)(2,1)S(1)}, bf16[256,512]{1,0:T(8,128)(2,1)S(1)}, f32[256,512]{1,0:T(8,128)S(1)}, f32[256,512]{1,0:T(8,128)S(1)}) custom-call(s32[1]{0:T(128)} %bitcast.1.core_ref, f32[64,128]{1,0:T(8,128)S(1)} %bitcast.30, f32[256,512]{1,0:T(8,128)S(1)} %get-tuple-element.45.att_ref, ...), custom_call_target="tpu_custom_call" | custom-call | flops 402653184 | bytes 4718592 | tf_op jit(solution)/shard_map/pallas_call | solution.py:286
  83.8 4.4 %all_gather.14.sent_ref = bf16[512,512]{1,0:T(8,128)(2,1)S(1)} all-gather(bf16[256,512]{1,0:T(8,128)(2,1)S(1)} %get-tuple-element.50), channel_id=1, replica_groups=mesh['x'=4,'zh'=4,'zl'=4,'core'=2,'head'=4] {'core'}, dimensions={0}, use_global_device_ids=true | all-gather | bytes 786432 | tf_op jit(solution)/shard_map/all_gather | solution.py:251
  88.2 0.8 shard_map.95
  89.1 0.0 all-to-all-done.5
  89.1 0.1 shard_map.93
  89.1 9.8 %all_to_all.81 = bf16[16,32,128]{2,1,0:T(8,128)(2,1)S(1)} all-to-all(bf16[16,32,128]{2,1,0:T(8,128)(2,1)S(1)} %bitcast.27), channel_id=1, replica_groups={{272,264,280,256,144,136,152,128,400,392,408,384,16,8,24,0},{273,265,28..., dimensions={0} | all-to-all | bytes 262144 | tf_op jit(solution)/shard_map/all_to_all | solution.py:235
  98.9 0.4 shard_map.96
  99.3 3.7 %all_gather.15.sent_ref = bf16[512,512]{1,0:T(8,128)(2,1)S(1)} all-gather(bf16[256,512]{1,0:T(8,128)(2,1)S(1)} %get-tuple-element.59), channel_id=1, replica_groups=mesh['x'=4,'zh'=4,'zl'=4,'core'=2,'head'=4] {'core'}, dimensions={0}, use_global_device_ids=true | all-gather | bytes 786432 | tf_op jit(solution)/shard_map/all_gather | solution.py:251
  103.0 0.8 shard_map.97
Async XLA Ops:
  0.6 1.0 copy-start
  1.6 0.9 copy-start.1
  20.8 12.9 %copy-start.2 = (bf16[128,1024]{1,0:T(8,128)(2,1)S(1)}, bf16[128,1024]{1,0:T(8,128)(2,1)}, u32[]{:S(2)}) copy-start(bf16[128,1024]{1,0:T(8,128)(2,1)} %q_ref.1) | copy-start | bytes 786436
  20.8 12.9 %copy-start.3 = (bf16[128,1024]{1,0:T(8,128)(2,1)S(1)}, bf16[128,1024]{1,0:T(8,128)(2,1)}, u32[]{:S(2)}) copy-start(bf16[128,1024]{1,0:T(8,128)(2,1)} %c_ref.1) | copy-start | bytes 786436
  21.4 17.7 %all-to-all-start.1 = ((bf16[4,128,128]{2,1,0:T(8,128)(2,1)}), bf16[4,128,128]{2,1,0:T(8,128)(2,1)S(1)}, u32[]{:S(2)}, u32[]{:S(2)}) async-start(bf16[4,128,128]{2,1,0:T(8,128)(2,1)} %bitcast.4), calls=%async_computation.1 | async-start | bytes 262144 | tf_op jit(solution)/shard_map/all_to_all | solution.py:243
  37.8 0.7 copy-start.4
  70.8 18.2 %all-to-all-start.5 = ((bf16[4,128,128]{2,1,0:T(8,128)(2,1)}), bf16[4,128,128]{2,1,0:T(8,128)(2,1)S(1)}, u32[]{:S(2)}, u32[]{:S(2)}) async-start(bf16[4,128,128]{2,1,0:T(8,128)(2,1)} %bitcast.13), calls=%async_computation.5 | async-start | bytes 262144 | tf_op jit(solution)/shard_map/all_to_all | solution.py:243
